TPU v7x, 32 devices: a whole 2x2x4 slice. The times are simulated.
32 devices in a mesh: sub: 8 (over z, y), grp: 4 (over x, core).
Axes of the slice: x: 2, y: 2, z: 4, core: 2. Of those that a mesh axis runs over, the one named last changes fastest.
Arguments:
- deflation: bfloat16 [512, 32, 4, 128], P(None, 'sub', 'grp'), may hold values from -0.045643546 to 0.045643546
- shift_field: float32 [32, 4, 128], P('sub', 'grp'), may hold values from 0.5 to 8
- counts: int32 [8], P('sub'), may hold values from 128 to 512, as said below
- right_sides: float32 [4096, 256], P(('sub', 'grp')), may hold values from -6 to 6
Outputs:
- coarse_solution: float32 [4096, 256], P(('sub', 'grp'))
Inputs may be any that keep to these rules, and one draw needn't show every extreme that they name: `counts`: live deflation vectors of each subdomain; some subdomain has 512 and some 512 // 4.
All inputs are finite; a program needn't handle non-finite values.
Results may differ from a plain program's by a relative error of at most 0.0014.
Values may be sent and summed in bfloat16 or wider, within the bound.
A program may use at most 64 MiB of HBM per device.

v0:
```python
import jax
import jax.numpy as jnp
from jax import lax
from jax.sharding import PartitionSpec as P

SWEEPS = 6


damping = 0.7


def extended(cells, sides, width):
    for axis, dim in sides:
        count = lax.axis_size(axis)
        ends = count - 1
        head = lax.slice_in_dim(cells, 0, width, axis=dim)
        tail = lax.slice_in_dim(cells, cells.shape[dim] - width, cells.shape[dim], axis=dim)
        cells = jnp.concatenate(
            [
                lax.ppermute(tail, axis, [(i, (i + 1) % count) for i in range(ends)]),
                cells,
                lax.ppermute(head, axis, [((i + 1) % count, i) for i in range(ends)]),
            ],
            axis=dim,
        )
    return cells


def smooth_last(values):
    width_x = values.shape[-1]
    positions = lax.iota(jnp.int32, width_x)
    left_side = jnp.where(positions >= 1, jnp.roll(values, 1, axis=-1), 0.0)
    right_side = jnp.where(positions < width_x - 1, jnp.roll(values, -1, axis=-1), 0.0)
    return values + 0.5 * (left_side + right_side)


def smooth_valid(values, which_axis):
    length = values.shape[which_axis]
    center = lax.slice_in_dim(values, 1, length - 1, axis=which_axis)
    lower = lax.slice_in_dim(values, 0, length - 2, axis=which_axis)
    upper = lax.slice_in_dim(values, 2, length, axis=which_axis)
    return center + 0.5 * (lower + upper)


def contract(left_part, right_part):
    return lax.dot_general(
        left_part, right_part, (((1,), (1,)), ((), ())), preferred_element_type=jnp.float32
    )


def on_device(deflation, shift_field, counts, right_sides):
    slot_count = deflation.shape[0]
    planes = deflation.shape[1]
    block_rows = right_sides.shape[0]
    live_count = counts[0]
    slot_ids = lax.iota(jnp.int32, slot_count)
    live_slots = slot_ids < live_count
    masked = jnp.where(live_slots[:, None, None, None], deflation, jnp.zeros((), deflation.dtype))
    padded = extended(masked, (("sub", 1), ("grp", 2)), 1)
    along_x = smooth_last(padded.astype(jnp.float32))
    along_y = smooth_valid(along_x, 2)
    inner_part = along_y[:, 1 : planes + 1]
    with_rims = jnp.pad(inner_part, ((0, 0), (1, 1), (0, 0), (0, 0)))
    along_z = smooth_valid(with_rims, 1)
    own_field = masked.astype(jnp.float32)
    images = ((16.0 + shift_field) * own_field - 2.0 * along_z).astype(jnp.bfloat16)
    above_plane = along_y[:, planes + 1].astype(jnp.bfloat16).reshape(slot_count, -1)
    below_plane = along_y[:, 0].astype(jnp.bfloat16).reshape(slot_count, -1)
    flat_vectors = masked.reshape(slot_count, -1)
    flat_images = images.reshape(slot_count, -1)
    top_plane = masked[:, planes - 1].reshape(slot_count, -1)
    bottom = masked[:, 0].reshape(slot_count, -1)
    row_start = lax.axis_index("grp") * block_rows
    lower_part = -contract(bottom, below_plane)
    middle = contract(flat_vectors, flat_images)
    upper_part = -contract(top_plane, above_plane)
    own_rows = lax.psum_scatter(
        jnp.concatenate([lower_part, middle, upper_part], axis=1),
        "grp",
        scatter_dimension=0,
        tiled=True,
    )
    row_slot = row_start + lax.iota(jnp.int32, block_rows)
    row_padded = row_slot >= live_count
    columns = lax.iota(jnp.int32, 3 * slot_count)
    pad_mask = (columns[None, :] == row_slot[:, None] + slot_count) & row_padded[:, None]
    matrix = own_rows + jnp.where(pad_mask, 1.0, 0.0).astype(jnp.float32)
    block = lax.dynamic_slice_in_dim(matrix, slot_count + row_start, block_rows, 1)
    factor = jnp.linalg.cholesky(block)
    rhs_masked = jnp.where(row_padded[:, None], 0.0, right_sides)
    current = damping * jax.scipy.linalg.cho_solve((factor, True), rhs_masked)
    for sweep in range(SWEEPS - 1):
        slab_iter = lax.all_gather(current, "grp", axis=0, tiled=True)
        stacked = extended(slab_iter, (("sub", 0),), slot_count)
        product = jnp.dot(matrix, stacked, precision=lax.Precision.HIGHEST)
        update = jax.scipy.linalg.cho_solve((factor, True), rhs_masked - product)
        current = current + damping * update
    return current


def solution(mesh):
    in_specs = (
        P(None, "sub", "grp", None),
        P("sub", "grp", None),
        P("sub"),
        P(("sub", "grp"), None),
    )
    out_specs = P(("sub", "grp"), None)
    return jax.shard_map(
        on_device, mesh=mesh, in_specs=in_specs, out_specs=out_specs, check_vma=False
    )
```

profile of v0, /device:TPU:17, one launch (start us, length us, event | category | flops | bytes accessed | tf_op | source)
XLA Modules:
  0.0 307.7 jit_solution(4979607070990679965)
XLA Ops:
  7.2 1.2 copy_select_fusion
  8.4 3.1 %collective-permute-start = (bf16[512,1,1,128]{3,0,2,1:T(8,128)(2,1)S(1)}, bf16[512,1,1,128]{3,0,2,1:T(8,128)(2,1)S(1)}, u32[]{:S(2)}, u32[]{:S(2)}) collective-permute-start(bf16[512,1,1,128]{3,0,2,1:T(8,128)(2,1)S(1)} %get-tuple-element.12), channel_id=1, source_target_pairs={{0,4},{4,8},{8,12},{12,16},{16,20},{20,24},{24,28},{1,5},{5,9},{9,... | collective-permute-start | bytes 393224 | tf_op jit(solution)/shard_map/ppermute | solution.py:20
  11.6 3.0 collective-permute-start.1
  14.6 1.0 collective-permute-done
  15.6 3.0 collective-permute-done.1
  18.7 4.3 %collective-permute-start.2 = (bf16[512,6,1,128]{3,0,2,1:T(8,128)(2,1)S(1)}, bf16[512,6,1,128]{3,0,2,1:T(8,128)(2,1)}, u32[]{:S(2)}, u32[]{:S(2)}) collective-permute-start(bf16[512,6,1,128]{3,0,2,1:T(8,128)(2,1)S(1)} %pad_maximum_fusion.1), channel_id=1, source_target_pairs={{0,1},{1,2},{2,3},{4,5},{5,6},{6,7},{8,9},{9,10},{10,11},{12,13},{... | collective-permute-start | bytes 2359304 | tf_op jit(solution)/shard_map/ppermute | solution.py:20
  23.1 1.9 collective-permute-start.3
  25.0 6.9 %collective-permute-done.2 = bf16[512,6,1,128]{3,0,2,1:T(8,128)(2,1)} collective-permute-done((bf16[512,6,1,128]{3,0,2,1:T(8,128)(2,1)S(1)}, bf16[512,6,1,128]{3,0,2,1:T(8,128)(2,1)}, u32[]{:S(2)}, u32[]{:S(2)}) %collective-permute-start.2) | collective-permute-done | bytes 786464 | tf_op jit(solution)/shard_map/ppermute | solution.py:20
  32.0 4.5 %collective-permute-done.3 = bf16[512,6,1,128]{3,0,2,1:T(8,128)(2,1)} collective-permute-done((bf16[512,6,1,128]{3,0,2,1:T(8,128)(2,1)S(1)}, bf16[512,6,1,128]{3,0,2,1:T(8,128)(2,1)}, u32[]{:S(2)}, u32[]{:S(2)}) %collective-permute-start.3) | collective-permute-done | bytes 786464 | tf_op jit(solution)/shard_map/ppermute | solution.py:22
  36.5 1.6 maximum_convert_fusion
  38.1 1.7 fusion.108
  39.8 3.8 %fusion.107 = (f32[512,6,3,127]{3,0,2,1:T(8,128)S(1)}, f32[512,6,3,127]{3,0,2,1:T(8,128)}) fusion(f32[512,6,3,128]{3,0,2,1:T(8,128)S(1)} %maximum_convert_fusion), kind=kLoop, calls=%fused_computation.129 | loop fusion | bytes 18726912 | tf_op jit(solution)/shard_map/jit(_roll_static)/slice | solution.py:33
  43.6 5.0 %fusion.2 = f32[512,6,3,128]{3,0,2,1:T(8,128)S(1)} fusion(f32[512,6,3,127]{3,0,2,1:T(8,128)} %get-tuple-element.9, f32[512,6,3,1]{3,0,2,1:T(8,128)S(1)} %get-tuple-element.11, f32[512,6,3,1]{3,0,2,1:T(8,128)S(1)} %get-tuple-element.10, f32[512,6,3,127]{3,0,2,1:T(8,128)S(1)} %get-tuple-element.8, pred[128]{0:T(512)(128)(4,1)S(1)} %get-tuple-element.14, ...), kind=kLoop, calls=%fused_computation.3 | loop fusion | flops 14155776 | bytes 16515328 | tf_op jit(solution)/shard_map/add | solution.py:34
  50.0 2.0 pad_maximum_fusion
  52.0 37.0 %reduce-scatter.2.cloned.1.call-done = f32[128,1536]{0,1:T(8,128)} async-done(((f32[512,1536]{0,1:T(8,128)}), f32[128,1536]{0,1:T(8,128)}) %reduce-scatter.2.cloned.1.call-update) | async-done | bytes 786448 | tf_op jit(solution)/shard_map/reduce_scatter | solution.py:77
  89.1 1.3 select_add_fusion
  90.5 11.7 %cholesky.18 = f32[128,128]{1,0:T(8,128)S(1)} custom-call(f32[128,128]{1,0:T(8,128)S(1)} %fusion.89), custom_call_target="Cholesky" | custom-call | tf_op jit(solution)/shard_map/jit(cholesky)/cholesky | solution.py:89
  103.6 9.8 %custom-call.13 = f32[1,128,128]{1,2,0:T(8,128)S(1)} custom-call(f32[1,128,128]{2,1,0:T(8,128)S(1)} %fusion.71), custom_call_target="InvertDiagBlocksLowerTriangular" | custom-call | tf_op jit(solution)/shard_map/jit(_cho_solve)/triangular_solve | solution.py:91
  114.0 7.3 %all_gather.15 = f32[512,256]{1,0:T(8,128)S(1)} all-gather(f32[128,256]{1,0:T(8,128)S(1)} %convolution_multiply_fusion.5), channel_id=1, replica_groups=mesh['sub'=8,'grp'=4] {'grp'}, dimensions={0}, use_global_device_ids=true | all-gather | bytes 655360 | tf_op jit(solution)/shard_map/all_gather | solution.py:93
  121.3 3.1 %collective-permute-start.4 = (f32[512,256]{1,0:T(8,128)S(1)}, f32[512,256]{1,0:T(8,128)S(1)}, u32[]{:S(2)}, u32[]{:S(2)}) collective-permute-start(f32[512,256]{1,0:T(8,128)S(1)} %all_gather.15), channel_id=1, source_target_pairs={{0,4},{4,8},{8,12},{12,16},{16,20},{20,24},{24,28},{1,5},{5,9},{9,... | collective-permute-start | bytes 1572872 | tf_op jit(solution)/shard_map/ppermute | solution.py:20
  124.4 3.1 %collective-permute-start.5 = (f32[512,256]{1,0:T(8,128)S(1)}, f32[512,256]{1,0:T(8,128)S(1)}, u32[]{:S(2)}, u32[]{:S(2)}) collective-permute-start(f32[512,256]{1,0:T(8,128)S(1)} %all_gather.15), channel_id=1, source_target_pairs={{4,0},{8,4},{12,8},{16,12},{20,16},{24,20},{28,24},{5,1},{9,5},{13... | collective-permute-start | bytes 1572872 | tf_op jit(solution)/shard_map/ppermute | solution.py:22
  127.5 19.3 %collective-permute-done.4 = f32[512,256]{1,0:T(8,128)S(1)} collective-permute-done((f32[512,256]{1,0:T(8,128)S(1)}, f32[512,256]{1,0:T(8,128)S(1)}, u32[]{:S(2)}, u32[]{:S(2)}) %collective-permute-start.4) | collective-permute-done | bytes 524320 | tf_op jit(solution)/shard_map/ppermute | solution.py:20
  146.8 2.4 collective-permute-done.5
  149.2 1.5 fusion.47
  151.2 7.3 %all_gather.16 = f32[512,256]{1,0:T(8,128)S(1)} all-gather(f32[128,256]{1,0:T(8,128)S(1)} %fusion.50), channel_id=1, replica_groups=mesh['sub'=8,'grp'=4] {'grp'}, dimensions={0}, use_global_device_ids=true | all-gather | bytes 655360 | tf_op jit(solution)/shard_map/all_gather | solution.py:93
  158.5 1.9 collective-permute-start.6
  160.5 4.5 %collective-permute-start.7 = (f32[512,256]{1,0:T(8,128)S(1)}, f32[512,256]{1,0:T(8,128)S(1)}, u32[]{:S(2)}, u32[]{:S(2)}) collective-permute-start(f32[512,256]{1,0:T(8,128)S(1)} %all_gather.16), channel_id=1, source_target_pairs={{4,0},{8,4},{12,8},{16,12},{20,16},{24,20},{28,24},{5,1},{9,5},{13... | collective-permute-start | bytes 1572872 | tf_op jit(solution)/shard_map/ppermute | solution.py:22
  164.9 18.0 %collective-permute-done.6 = f32[512,256]{1,0:T(8,128)S(1)} collective-permute-done((f32[512,256]{1,0:T(8,128)S(1)}, f32[512,256]{1,0:T(8,128)S(1)}, u32[]{:S(2)}, u32[]{:S(2)}) %collective-permute-start.6) | collective-permute-done | bytes 524320 | tf_op jit(solution)/shard_map/ppermute | solution.py:20
  182.9 3.5 %collective-permute-done.7 = f32[512,256]{1,0:T(8,128)S(1)} collective-permute-done((f32[512,256]{1,0:T(8,128)S(1)}, f32[512,256]{1,0:T(8,128)S(1)}, u32[]{:S(2)}, u32[]{:S(2)}) %collective-permute-start.7) | collective-permute-done | bytes 524320 | tf_op jit(solution)/shard_map/ppermute | solution.py:22
  186.4 1.5 fusion.44
  188.5 7.3 %all_gather.17 = f32[512,256]{1,0:T(8,128)S(1)} all-gather(f32[128,256]{1,0:T(8,128)S(1)} %fusion.51), channel_id=1, replica_groups=mesh['sub'=8,'grp'=4] {'grp'}, dimensions={0}, use_global_device_ids=true | all-gather | bytes 655360 | tf_op jit(solution)/shard_map/all_gather | solution.py:93
  195.8 1.9 collective-permute-start.8
  197.7 4.3 %collective-permute-start.9 = (f32[512,256]{1,0:T(8,128)S(1)}, f32[512,256]{1,0:T(8,128)S(1)}, u32[]{:S(2)}, u32[]{:S(2)}) collective-permute-start(f32[512,256]{1,0:T(8,128)S(1)} %all_gather.17), channel_id=1, source_target_pairs={{4,0},{8,4},{12,8},{16,12},{20,16},{24,20},{28,24},{5,1},{9,5},{13... | collective-permute-start | bytes 1572872 | tf_op jit(solution)/shard_map/ppermute | solution.py:22
  202.0 18.3 %collective-permute-done.8 = f32[512,256]{1,0:T(8,128)S(1)} collective-permute-done((f32[512,256]{1,0:T(8,128)S(1)}, f32[512,256]{1,0:T(8,128)S(1)}, u32[]{:S(2)}, u32[]{:S(2)}) %collective-permute-start.8) | collective-permute-done | bytes 524320 | tf_op jit(solution)/shard_map/ppermute | solution.py:20
  220.3 3.4 %collective-permute-done.9 = f32[512,256]{1,0:T(8,128)S(1)} collective-permute-done((f32[512,256]{1,0:T(8,128)S(1)}, f32[512,256]{1,0:T(8,128)S(1)}, u32[]{:S(2)}, u32[]{:S(2)}) %collective-permute-start.9) | collective-permute-done | bytes 524320 | tf_op jit(solution)/shard_map/ppermute | solution.py:22
  223.7 1.5 fusion.41
  225.7 7.3 %all_gather.18 = f32[512,256]{1,0:T(8,128)S(1)} all-gather(f32[128,256]{1,0:T(8,128)S(1)} %fusion.52), channel_id=1, replica_groups=mesh['sub'=8,'grp'=4] {'grp'}, dimensions={0}, use_global_device_ids=true | all-gather | bytes 655360 | tf_op jit(solution)/shard_map/all_gather | solution.py:93
  233.0 1.9 collective-permute-start.10
  235.0 4.3 %collective-permute-start.11 = (f32[512,256]{1,0:T(8,128)S(1)}, f32[512,256]{1,0:T(8,128)S(1)}, u32[]{:S(2)}, u32[]{:S(2)}) collective-permute-start(f32[512,256]{1,0:T(8,128)S(1)} %all_gather.18), channel_id=1, source_target_pairs={{4,0},{8,4},{12,8},{16,12},{20,16},{24,20},{28,24},{5,1},{9,5},{13... | collective-permute-start | bytes 1572872 | tf_op jit(solution)/shard_map/ppermute | solution.py:22
  239.2 18.3 %collective-permute-done.10 = f32[512,256]{1,0:T(8,128)S(1)} collective-permute-done((f32[512,256]{1,0:T(8,128)S(1)}, f32[512,256]{1,0:T(8,128)S(1)}, u32[]{:S(2)}, u32[]{:S(2)}) %collective-permute-start.10) | collective-permute-done | bytes 524320 | tf_op jit(solution)/shard_map/ppermute | solution.py:20
  257.6 3.4 %collective-permute-done.11 = f32[512,256]{1,0:T(8,128)S(1)} collective-permute-done((f32[512,256]{1,0:T(8,128)S(1)}, f32[512,256]{1,0:T(8,128)S(1)}, u32[]{:S(2)}, u32[]{:S(2)}) %collective-permute-start.11) | collective-permute-done | bytes 524320 | tf_op jit(solution)/shard_map/ppermute | solution.py:22
  260.9 1.5 fusion.38
  263.0 7.3 %all_gather.19 = f32[512,256]{1,0:T(8,128)S(1)} all-gather(f32[128,256]{1,0:T(8,128)S(1)} %fusion.53), channel_id=1, replica_groups=mesh['sub'=8,'grp'=4] {'grp'}, dimensions={0}, use_global_device_ids=true | all-gather | bytes 655360 | tf_op jit(solution)/shard_map/all_gather | solution.py:93
  270.3 1.9 collective-permute-start.12
  272.2 4.3 %collective-permute-start.13 = (f32[512,256]{1,0:T(8,128)S(1)}, f32[512,256]{1,0:T(8,128)S(1)}, u32[]{:S(2)}, u32[]{:S(2)}) collective-permute-start(f32[512,256]{1,0:T(8,128)S(1)} %all_gather.19), channel_id=1, source_target_pairs={{4,0},{8,4},{12,8},{16,12},{20,16},{24,20},{28,24},{5,1},{9,5},{13... | collective-permute-start | bytes 1572872 | tf_op jit(solution)/shard_map/ppermute | solution.py:22
  276.5 18.3 %collective-permute-done.12 = f32[512,256]{1,0:T(8,128)S(1)} collective-permute-done((f32[512,256]{1,0:T(8,128)S(1)}, f32[512,256]{1,0:T(8,128)S(1)}, u32[]{:S(2)}, u32[]{:S(2)}) %collective-permute-start.12) | collective-permute-done | bytes 524320 | tf_op jit(solution)/shard_map/ppermute | solution.py:20
  294.8 3.4 %collective-permute-done.13 = f32[512,256]{1,0:T(8,128)S(1)} collective-permute-done((f32[512,256]{1,0:T(8,128)S(1)}, f32[512,256]{1,0:T(8,128)S(1)}, u32[]{:S(2)}, u32[]{:S(2)}) %collective-permute-start.13) | collective-permute-done | bytes 524320 | tf_op jit(solution)/shard_map/ppermute | solution.py:22
  298.2 1.5 fusion.35
  (40 shorter events, 7.2 us)
Async XLA Ops:
  6.5 18.5 %copy-start.3 = (f32[4,1,128]{2,1,0:T(1,128)S(1)}, f32[4,1,128]{2,1,0:T(1,128)}, u32[]{:S(2)}) copy-start(f32[4,1,128]{2,1,0:T(1,128)} %param.7) | copy-start | bytes 6148
  6.5 82.5 %reduce-scatter.2.cloned.1.call-start = ((), (), s32[]{:S(2)}) async-start(), calls=%async_computation.1 | async-start | bytes 3932160 | tf_op jit(solution)/shard_map/reduce_scatter | solution.py:77
  8.4 7.2 %collective-permute-start = (bf16[512,1,1,128]{3,0,2,1:T(8,128)(2,1)S(1)}, bf16[512,1,1,128]{3,0,2,1:T(8,128)(2,1)S(1)}, u32[]{:S(2)}, u32[]{:S(2)}) collective-permute-start(bf16[512,1,1,128]{3,0,2,1:T(8,128)(2,1)S(1)} %get-tuple-element.12), channel_id=1, source_target_pairs={{0,4},{4,8},{8,12},{12,16},{16,20},{20,24},{24,28},{1,5},{5,9},{9,... | collective-permute-start | bytes 393224 | tf_op jit(solution)/shard_map/ppermute | solution.py:20
  11.6 7.0 %collective-permute-start.1 = (bf16[512,1,1,128]{3,0,2,1:T(8,128)(2,1)S(1)}, bf16[512,1,1,128]{3,0,2,1:T(8,128)(2,1)S(1)}, u32[]{:S(2)}, u32[]{:S(2)}) collective-permute-start(bf16[512,1,1,128]{3,0,2,1:T(8,128)(2,1)S(1)} %get-tuple-element.13), channel_id=1, source_target_pairs={{4,0},{8,4},{12,8},{16,12},{20,16},{24,20},{28,24},{5,1},{9,5},{13... | collective-permute-start | bytes 393224 | tf_op jit(solution)/shard_map/ppermute | solution.py:22
  15.6 20.9 %copy-start.1 = (bf16[512,1,1,128]{3,0,2,1:T(8,128)(2,1)}, bf16[512,1,1,128]{3,0,2,1:T(8,128)(2,1)S(1)}, u32[]{:S(2)}) copy-start(bf16[512,1,1,128]{3,0,2,1:T(8,128)(2,1)S(1)} %collective-permute-done) | copy-start | bytes 393220
  18.6 17.9 %copy-start.2 = (bf16[512,1,1,128]{3,0,2,1:T(8,128)(2,1)}, bf16[512,1,1,128]{3,0,2,1:T(8,128)(2,1)S(1)}, u32[]{:S(2)}) copy-start(bf16[512,1,1,128]{3,0,2,1:T(8,128)(2,1)S(1)} %collective-permute-done.1) | copy-start | bytes 393220
  18.7 13.2 %collective-permute-start.2 = (bf16[512,6,1,128]{3,0,2,1:T(8,128)(2,1)S(1)}, bf16[512,6,1,128]{3,0,2,1:T(8,128)(2,1)}, u32[]{:S(2)}, u32[]{:S(2)}) collective-permute-start(bf16[512,6,1,128]{3,0,2,1:T(8,128)(2,1)S(1)} %pad_maximum_fusion.1), channel_id=1, source_target_pairs={{0,1},{1,2},{2,3},{4,5},{5,6},{6,7},{8,9},{9,10},{10,11},{12,13},{... | collective-permute-start | bytes 2359304 | tf_op jit(solution)/shard_map/ppermute | solution.py:20
  23.1 13.4 %collective-permute-start.3 = (bf16[512,6,1,128]{3,0,2,1:T(8,128)(2,1)S(1)}, bf16[512,6,1,128]{3,0,2,1:T(8,128)(2,1)}, u32[]{:S(2)}, u32[]{:S(2)}) collective-permute-start(bf16[512,6,1,128]{3,0,2,1:T(8,128)(2,1)S(1)} %pad_maximum_fusion.1), channel_id=1, source_target_pairs={{1,0},{2,1},{3,2},{5,4},{6,5},{7,6},{9,8},{10,9},{11,10},{13,12},{... | collective-permute-start | bytes 2359304 | tf_op jit(solution)/shard_map/ppermute | solution.py:22
  52.0 61.4 %copy-start = (f32[128,256]{1,0:T(8,128)S(1)}, f32[128,256]{1,0:T(8,128)}, u32[]{:S(2)}) copy-start(f32[128,256]{1,0:T(8,128)} %param.9) | copy-start | bytes 393220
  121.3 25.5 %collective-permute-start.4 = (f32[512,256]{1,0:T(8,128)S(1)}, f32[512,256]{1,0:T(8,128)S(1)}, u32[]{:S(2)}, u32[]{:S(2)}) collective-permute-start(f32[512,256]{1,0:T(8,128)S(1)} %all_gather.15), channel_id=1, source_target_pairs={{0,4},{4,8},{8,12},{12,16},{16,20},{20,24},{24,28},{1,5},{5,9},{9,... | collective-permute-start | bytes 1572872 | tf_op jit(solution)/shard_map/ppermute | solution.py:20
  124.4 24.8 %collective-permute-start.5 = (f32[512,256]{1,0:T(8,128)S(1)}, f32[512,256]{1,0:T(8,128)S(1)}, u32[]{:S(2)}, u32[]{:S(2)}) collective-permute-start(f32[512,256]{1,0:T(8,128)S(1)} %all_gather.15), channel_id=1, source_target_pairs={{4,0},{8,4},{12,8},{16,12},{20,16},{24,20},{28,24},{5,1},{9,5},{13... | collective-permute-start | bytes 1572872 | tf_op jit(solution)/shard_map/ppermute | solution.py:22
  158.5 24.4 %collective-permute-start.6 = (f32[512,256]{1,0:T(8,128)S(1)}, f32[512,256]{1,0:T(8,128)S(1)}, u32[]{:S(2)}, u32[]{:S(2)}) collective-permute-start(f32[512,256]{1,0:T(8,128)S(1)} %all_gather.16), channel_id=1, source_target_pairs={{0,4},{4,8},{8,12},{12,16},{16,20},{20,24},{24,28},{1,5},{5,9},{9,... | collective-permute-start | bytes 1572872 | tf_op jit(solution)/shard_map/ppermute | solution.py:20
  160.5 26.0 %collective-permute-start.7 = (f32[512,256]{1,0:T(8,128)S(1)}, f32[512,256]{1,0:T(8,128)S(1)}, u32[]{:S(2)}, u32[]{:S(2)}) collective-permute-start(f32[512,256]{1,0:T(8,128)S(1)} %all_gather.16), channel_id=1, source_target_pairs={{4,0},{8,4},{12,8},{16,12},{20,16},{24,20},{28,24},{5,1},{9,5},{13... | collective-permute-start | bytes 1572872 | tf_op jit(solution)/shard_map/ppermute | solution.py:22
  195.8 24.5 %collective-permute-start.8 = (f32[512,256]{1,0:T(8,128)S(1)}, f32[512,256]{1,0:T(8,128)S(1)}, u32[]{:S(2)}, u32[]{:S(2)}) collective-permute-start(f32[512,256]{1,0:T(8,128)S(1)} %all_gather.17), channel_id=1, source_target_pairs={{0,4},{4,8},{8,12},{12,16},{16,20},{20,24},{24,28},{1,5},{5,9},{9,... | collective-permute-start | bytes 1572872 | tf_op jit(solution)/shard_map/ppermute | solution.py:20
  197.7 26.0 %collective-permute-start.9 = (f32[512,256]{1,0:T(8,128)S(1)}, f32[512,256]{1,0:T(8,128)S(1)}, u32[]{:S(2)}, u32[]{:S(2)}) collective-permute-start(f32[512,256]{1,0:T(8,128)S(1)} %all_gather.17), channel_id=1, source_target_pairs={{4,0},{8,4},{12,8},{16,12},{20,16},{24,20},{28,24},{5,1},{9,5},{13... | collective-permute-start | bytes 1572872 | tf_op jit(solution)/shard_map/ppermute | solution.py:22
  233.0 24.5 %collective-permute-start.10 = (f32[512,256]{1,0:T(8,128)S(1)}, f32[512,256]{1,0:T(8,128)S(1)}, u32[]{:S(2)}, u32[]{:S(2)}) collective-permute-start(f32[512,256]{1,0:T(8,128)S(1)} %all_gather.18), channel_id=1, source_target_pairs={{0,4},{4,8},{8,12},{12,16},{16,20},{20,24},{24,28},{1,5},{5,9},{9,... | collective-permute-start | bytes 1572872 | tf_op jit(solution)/shard_map/ppermute | solution.py:20
  235.0 26.0 %collective-permute-start.11 = (f32[512,256]{1,0:T(8,128)S(1)}, f32[512,256]{1,0:T(8,128)S(1)}, u32[]{:S(2)}, u32[]{:S(2)}) collective-permute-start(f32[512,256]{1,0:T(8,128)S(1)} %all_gather.18), channel_id=1, source_target_pairs={{4,0},{8,4},{12,8},{16,12},{20,16},{24,20},{28,24},{5,1},{9,5},{13... | collective-permute-start | bytes 1572872 | tf_op jit(solution)/shard_map/ppermute | solution.py:22
  270.3 24.5 %collective-permute-start.12 = (f32[512,256]{1,0:T(8,128)S(1)}, f32[512,256]{1,0:T(8,128)S(1)}, u32[]{:S(2)}, u32[]{:S(2)}) collective-permute-start(f32[512,256]{1,0:T(8,128)S(1)} %all_gather.19), channel_id=1, source_target_pairs={{0,4},{4,8},{8,12},{12,16},{16,20},{20,24},{24,28},{1,5},{5,9},{9,... | collective-permute-start | bytes 1572872 | tf_op jit(solution)/shard_map/ppermute | solution.py:20
  272.2 26.0 %collective-permute-start.13 = (f32[512,256]{1,0:T(8,128)S(1)}, f32[512,256]{1,0:T(8,128)S(1)}, u32[]{:S(2)}, u32[]{:S(2)}) collective-permute-start(f32[512,256]{1,0:T(8,128)S(1)} %all_gather.19), channel_id=1, source_target_pairs={{4,0},{8,4},{12,8},{16,12},{20,16},{24,20},{28,24},{5,1},{9,5},{13... | collective-permute-start | bytes 1572872 | tf_op jit(solution)/shard_map/ppermute | solution.py:22
Sparse Core Ops, SparseCore 0:
  52.1 36.9 reduce-scatter.1
where the time goes:
time: 308 us
  waiting for transfers between devices  161 us (52%)
  starting transfers between devices  43.5 us (14%)
  blocking collectives  36.5 us (12%)
  other arithmetic  34.3 us (11%)
  between operations  14.5 us (5%)
  matrix products  12.5 us (4%)
  local copies, waits for them, and re-layouts  5.69 us (2%)
    ppermute x7, waiting for transfers between devices, extended(): lax.ppermute(tail, axis, [(i, (i + 1) % count) for i in range(ends)])  100 us
    reduce_scatter x1, waiting for transfers between devices, on_device(): lax.psum_scatter(jnp.concatenate([lower_part, middle, upper_part], axis=1...  37 us
    all_gather x5, blocking collectives, on_device(): slab_iter = lax.all_gather(current, 'grp', axis=0, tiled=True)  36.5 us
    ppermute x7, starting transfers between devices, extended(): lax.ppermute(head, axis, [((i + 1) % count, i) for i in range(ends)])  25.3 us
    ppermute x7, waiting for transfers between devices, extended(): lax.ppermute(head, axis, [((i + 1) % count, i) for i in range(ends)])  23.6 us
    ppermute x7, starting transfers between devices, extended(): lax.ppermute(tail, axis, [(i, (i + 1) % count) for i in range(ends)])  18.2 us
    another operation x3, other arithmetic, on_device(): factor = jnp.linalg.cholesky(block)  12.4 us
    another operation x2, other arithmetic, on_device(): current = damping * jax.scipy.linalg.cho_solve((factor, True), rhs_masked)  10.5 us
  transfers between devices with their start and end apart: 15, of which 15 were waited for; matrix products, arithmetic and copies ran while one was open for 0% of the time, Pallas kernels for 0%

commit v1 on v0

v1 whole, which is shorter than its diff:
```python
import functools

import jax
import jax.numpy as jnp
import numpy as np
from jax import lax
from jax.experimental import pallas as pl
from jax.experimental.pallas import tpu as pltpu
from jax.sharding import PartitionSpec as P

SWEEPS = 6
damping = 0.7
HIGHEST = lax.Precision.HIGHEST


def remote(src, dst, send_sem, recv_sem, device):
    return pltpu.make_async_remote_copy(
        src_ref=src,
        dst_ref=dst,
        send_sem=send_sem,
        recv_sem=recv_sem,
        device_id=device,
        device_id_type=pl.DeviceIdType.MESH,
    )


def place(subs):
    s, g = lax.axis_index("sub"), lax.axis_index("grp")
    far = g + 2 - 4 * (g // 2)
    near = g + 1 - 2 * lax.rem(g, 2)
    corner = near + 2 - 4 * (near // 2)
    return s, g, far, near, corner, s > 0, s < subs - 1


def greet(s, g, far, near, has_low, has_high):
    barrier = pltpu.get_barrier_semaphore()

    def signal(device):
        pl.semaphore_signal(
            barrier, inc=1, device_id=device, device_id_type=pl.DeviceIdType.MESH
        )

    signal((s, far))
    signal((s, near))

    @pl.when(has_low)
    def _():
        signal((s - 1, g))

    @pl.when(has_high)
    def _():
        signal((s + 1, g))

    peers = 2 + has_low.astype(jnp.int32) + has_high.astype(jnp.int32)
    pl.semaphore_wait(barrier, peers)


def against(left_part, right_part):
    return lax.dot_general(
        left_part, right_part, (((1,), (1,)), ((), ())), preferred_element_type=jnp.float32
    )


def setup_kernel(
    subs, planes, z_ref, shift_ref, spread_ref, pad_ref, e_ref,
    zall, rims, shifts, along, z_send, z_recv, rim_send, rim_recv, sh_send, sh_recv,
):
    s, g, far, near, corner, has_low, has_high = place(subs)
    groups, slots, cells = zall.shape
    width = cells // planes
    own = slots // groups
    chunks = z_recv.shape[1]
    step = slots // chunks

    zall[g] = z_ref[...]
    shifts[g] = shift_ref[...]
    greet(s, g, far, near, has_low, has_high)

    def z_copy(slot, part, kind, to):
        ref = zall.at[slot, pl.ds(part * step, step)]
        return remote(ref, ref, z_send.at[kind, part], z_recv.at[slot, part], (s, to))

    def sh_copy(slot, kind, to):
        ref = shifts.at[slot]
        return remote(ref, ref, sh_send.at[kind], sh_recv.at[slot], (s, to))

    def rim_first(side):
        plane = (planes - 1 if side == 0 else 0) * width
        to = s + 1 if side == 0 else s - 1
        return remote(
            zall.at[g, :, pl.ds(plane, width)], rims.at[side, g],
            rim_send.at[side, 0], rim_recv.at[side, g], (to, g),
        )

    def rim_copy(side, slot, kind, to):
        ref = rims.at[side, slot]
        return remote(ref, ref, rim_send.at[side, kind], rim_recv.at[side, slot], (s, to))

    sends = {0: has_high, 1: has_low}
    holds = {0: has_low, 1: has_high}

    sh_copy(g, 0, far).start()
    sh_copy(g, 1, near).start()
    for part in range(chunks):
        z_copy(g, part, 0, far).start()
    for side in (0, 1):
        @pl.when(sends[side])
        def _(side=side):
            rim_first(side).start()
    for part in range(chunks):
        z_copy(g, part, 1, near).start()

    sh_copy(far, 2, near).wait_recv()
    sh_copy(far, 2, near).start()
    for part in range(chunks):
        z_copy(far, part, 2, near).wait_recv()
        z_copy(far, part, 2, near).start()
    for side in (0, 1):
        @pl.when(holds[side])
        def _(side=side):
            rim_copy(side, g, 1, far).wait_recv()
            rim_copy(side, g, 1, far).start()
            rim_copy(side, g, 2, near).start()

    sh_copy(near, 2, near).wait_recv()
    sh_copy(corner, 2, near).wait_recv()
    for slot in (near, corner):
        for part in range(chunks):
            z_copy(slot, part, 2, near).wait_recv()

    mine = pl.ds(pl.multiple_of(g * own, own), own)
    for y in range(groups):
        along[y] = jnp.dot(zall[y], spread_ref[...], preferred_element_type=jnp.float32)
    total = jnp.zeros((own, slots), jnp.float32)
    for y in range(groups):
        beside = None
        for other in (y - 1, y + 1):
            if 0 <= other < groups:
                beside = along[other] if beside is None else beside + along[other]
        smooth = along[y] if beside is None else along[y] + 0.5 * beside
        centre = (16.0 + shifts[y][0:1, :]) * zall[y].astype(jnp.float32)
        image = (centre - 2.0 * smooth).astype(jnp.bfloat16)
        total = total + against(zall[y, mine, :], image)
    e_ref[:, pl.ds(slots, slots)] = total
    block = pl.ds(pl.multiple_of(slots + g * own, own), own)
    e_ref[:, block] = e_ref[:, block] + pad_ref[...]

    for side in (0, 1):
        @pl.when(holds[side])
        def _(side=side):
            rim_copy(side, far, 3, near).wait_recv()
            rim_copy(side, far, 3, near).start()
    for side in (0, 1):
        columns = pl.ds(2 * side * slots, slots)

        @pl.when(holds[side])
        def _(side=side, columns=columns):
            for slot in (near, corner):
                rim_copy(side, slot, 3, near).wait_recv()
            rows = [
                jnp.dot(
                    rims[side, y], spread_ref[0:width, 0:width],
                    preferred_element_type=jnp.float32,
                )
                for y in range(groups)
            ]
            plane = 0 if side == 0 else (planes - 1) * width
            part = jnp.zeros((own, slots), jnp.float32)
            for y in range(groups):
                beside = [rows[o] for o in (y - 1, y + 1) if 0 <= o < groups]
                smooth = rows[y] + 0.5 * sum(beside[1:], beside[0]) if beside else rows[y]
                part = part + against(
                    zall[y, mine, plane : plane + width], smooth.astype(jnp.bfloat16)
                )
            e_ref[:, columns] = -part

        @pl.when(jnp.logical_not(holds[side]))
        def _(columns=columns):
            e_ref[:, columns] = jnp.zeros((own, slots), jnp.float32)

    for kind in range(3):
        sh_copy(g, kind, far).wait_send()
        for part in range(chunks):
            z_copy(g, part, kind, far).wait_send()
    for side in (0, 1):
        @pl.when(sends[side])
        def _(side=side):
            rim_first(side).wait_send()

        @pl.when(holds[side])
        def _(side=side):
            for kind in (1, 2, 3):
                rim_copy(side, g, kind, far).wait_send()


def sweep_kernel(
    subs, e_ref, inverse_ref, b_ref, x_ref, matrix, held, change, sent, correction,
    send_sem, recv_sem,
):
    s, g, far, near, corner, has_low, has_high = place(subs)
    rows, width = b_ref.shape
    groups = held.shape[1] // 3
    sends = {0: has_high, 1: has_low}
    holds = {0: has_low, 1: has_high}
    start = {0: 0, 1: 2 * groups}
    depth = groups * rows

    def mix(at, kind, ref_slot, to):
        ref = held.at[at, ref_slot]
        return remote(ref, ref, send_sem.at[at, kind], recv_sem.at[at, ref_slot], to)

    def first(at, side):
        to = s + 1 if side == 0 else s - 1
        slot = start[side] + g
        return remote(
            held.at[at, groups + g], held.at[at, slot],
            send_sem.at[at, side], recv_sem.at[at, slot], (to, g),
        )

    greet(s, g, far, near, has_low, has_high)

    full = jnp.dot(inverse_ref[...], e_ref[...], precision=HIGHEST,
                   preferred_element_type=jnp.float32)
    high = full.astype(jnp.bfloat16)
    matrix[0:rows] = high
    matrix[rows : 2 * rows] = (full - high.astype(jnp.float32)).astype(jnp.bfloat16)
    begin = jnp.dot(inverse_ref[...], b_ref[...], precision=HIGHEST,
                    preferred_element_type=jnp.float32)
    correction[...] = begin
    x_ref[...] = damping * begin
    sent[...] = jnp.zeros_like(sent)

    def take(at, begin_slot):
        values = held[at, pl.ds(begin_slot, groups)].reshape(depth, width)
        columns = matrix[:, begin_slot * rows : (begin_slot + groups) * rows]
        both = jnp.dot(columns, values, preferred_element_type=jnp.float32)
        correction[...] = correction[...] - (both[0:rows] + both[rows:])

    def send(at):
        delta = (x_ref[...] - sent[...]).astype(jnp.bfloat16)
        sent[...] = sent[...] + delta.astype(jnp.float32)
        held[at, groups + g] = delta
        for side in (0, 1):
            @pl.when(sends[side])
            def _(side=side):
                first(at, side).start()
        mix(at, 2, groups + g, (s, far)).start()
        mix(at, 3, groups + g, (s, near)).start()

    def collect(at):
        mix(at, 4, groups + far, (s, near)).wait_recv()
        mix(at, 4, groups + far, (s, near)).start()
        for side in (0, 1):
            @pl.when(holds[side])
            def _(side=side):
                slot = start[side] + g
                mix(at, 5 + 3 * side, slot, (s, far)).wait_recv()
                mix(at, 5 + 3 * side, slot, (s, far)).start()
                mix(at, 6 + 3 * side, slot, (s, near)).start()
        for slot in (near, corner):
            mix(at, 4, groups + slot, (s, near)).wait_recv()
        take(at, groups)
        for side in (0, 1):
            @pl.when(holds[side])
            def _(side=side):
                slot = start[side] + far
                mix(at, 7 + 3 * side, slot, (s, near)).wait_recv()
                mix(at, 7 + 3 * side, slot, (s, near)).start()
        for side in (0, 1):
            @pl.when(holds[side])
            def _(side=side):
                for other in (near, corner):
                    mix(at, 7 + 3 * side, start[side] + other, (s, near)).wait_recv()
                take(at, start[side])

    def update():
        x_ref[...] = x_ref[...] + damping * correction[...]

    def sweep(at, carry):
        send(at)
        collect(at)
        update()
        return carry

    send(0)
    send(1)
    collect(0)
    collect(1)
    update()
    lax.fori_loop(2, SWEEPS, sweep, 0)

    def drain(at, carry):
        for kind in (2, 3, 4):
            mix(at, kind, groups + g, (s, far)).wait_send()
        for side in (0, 1):
            @pl.when(sends[side])
            def _(side=side):
                first(at, side).wait_send()

            @pl.when(holds[side])
            def _(side=side):
                for kind in (5, 6, 7):
                    mix(at, kind + 3 * side, groups + g, (s, far)).wait_send()
        return carry

    lax.fori_loop(0, SWEEPS, drain, 0)


def on_device(subs, groups, deflation, shift_field, counts, right_sides):
    slots, planes, _, width = deflation.shape
    rows, sides = right_sides.shape
    cells = planes * width
    live_count = counts[0]
    live_slots = lax.iota(jnp.int32, slots) < live_count
    masked = jnp.where(
        live_slots[:, None], deflation.reshape(slots, cells), jnp.zeros((), deflation.dtype)
    )
    shift = jnp.broadcast_to(shift_field.reshape(1, cells), (8, cells))

    def line(n):
        return np.eye(n) + 0.5 * (np.eye(n, k=1) + np.eye(n, k=-1))

    spread = jnp.asarray(np.kron(line(planes), line(width)), jnp.bfloat16)
    row_slot = lax.axis_index("grp") * rows + lax.iota(jnp.int32, rows)
    dead = row_slot >= live_count
    pad = jnp.where(dead[:, None], jnp.eye(rows, dtype=jnp.float32), 0.0)
    vmem = pl.BlockSpec(memory_space=pltpu.VMEM)
    chunks = 4
    bf16, f32 = jnp.bfloat16, jnp.float32
    matrix = pl.pallas_call(
        functools.partial(setup_kernel, subs, planes),
        out_shape=jax.ShapeDtypeStruct((rows, 3 * slots), f32),
        in_specs=[vmem] * 4,
        out_specs=vmem,
        scratch_shapes=[
            pltpu.VMEM((groups, slots, cells), bf16),
            pltpu.VMEM((2, groups, slots, width), bf16),
            pltpu.VMEM((groups, 8, cells), f32),
            pltpu.VMEM((groups, slots, cells), f32),
            pltpu.SemaphoreType.DMA((3, chunks)),
            pltpu.SemaphoreType.DMA((groups, chunks)),
            pltpu.SemaphoreType.DMA((2, 4)),
            pltpu.SemaphoreType.DMA((2, groups)),
            pltpu.SemaphoreType.DMA((3,)),
            pltpu.SemaphoreType.DMA((groups,)),
        ],
        compiler_params=pltpu.CompilerParams(
            collective_id=0, has_side_effects=True, vmem_limit_bytes=40 * 2**20
        ),
        name="coarse_rows",
    )(masked, shift, spread, pad)

    block = lax.dynamic_slice_in_dim(matrix, slots + lax.axis_index("grp") * rows, rows, 1)
    factor = jnp.linalg.cholesky(block)
    inverse = jax.scipy.linalg.cho_solve((factor, True), jnp.eye(rows, dtype=f32))
    rhs = jnp.where(dead[:, None], 0.0, right_sides)
    count = SWEEPS
    return pl.pallas_call(
        functools.partial(sweep_kernel, subs),
        out_shape=jax.ShapeDtypeStruct((rows, sides), f32),
        in_specs=[vmem] * 3,
        out_specs=vmem,
        scratch_shapes=[
            pltpu.VMEM((2 * rows, 3 * slots), bf16),
            pltpu.VMEM((count, 3 * groups, rows, sides), bf16),
            pltpu.VMEM((8, 128), f32),
            pltpu.VMEM((rows, sides), f32),
            pltpu.VMEM((rows, sides), f32),
            pltpu.SemaphoreType.DMA((count, 11)),
            pltpu.SemaphoreType.DMA((count, 3 * groups)),
        ],
        compiler_params=pltpu.CompilerParams(
            collective_id=1, has_side_effects=True, vmem_limit_bytes=40 * 2**20
        ),
        name="sweeps",
    )(matrix, inverse, rhs)


def solution(mesh):
    in_specs = (
        P(None, "sub", "grp", None),
        P("sub", "grp", None),
        P("sub"),
        P(("sub", "grp"), None),
    )
    out_specs = P(("sub", "grp"), None)
    return jax.shard_map(
        functools.partial(on_device, mesh.shape["sub"], mesh.shape["grp"]),
        mesh=mesh, in_specs=in_specs, out_specs=out_specs, check_vma=False,
    )
```

time: 308 us -> 111 us (0.36)
  waiting for transfers between devices: 161 us -> 0 us
  Pallas kernels: 0 us -> 84.2 us
  starting transfers between devices: 43.5 us -> 0 us
  blocking collectives: 36.5 us -> 0 us
  between operations: 14.5 us -> 0.8 us
  matrix products: 12.5 us -> 0.45 us
  other arithmetic: 34.3 us -> 24.3 us
  local copies, waits for them, and re-layouts: 5.69 us -> 1.47 us
    ppermute x14 -> x0, waiting for transfers between devices: 124 us -> none  [the longest x7 100 us: extended(): lax.ppermute(tail, axis, [(i, (i + 1) % count) for i in range(ends)])]
    pallas_call x0 -> x2, Pallas kernels: none -> 84.2 us  [the longest x1 60.6 us: on_device(): pl.pallas_call(functools.partial(sweep_kernel, subs), out_shape=jax.Shape...]
    ppermute x14 -> x0, starting transfers between devices: 43.5 us -> none  [the longest x7 25.3 us: extended(): lax.ppermute(head, axis, [((i + 1) % count, i) for i in range(ends)])]
    reduce_scatter x1 -> x0, waiting for transfers between devices: 37 us -> none  [on_device(): lax.psum_scatter(jnp.concatenate([lower_part, middle, upper_part], axis=1...]
    all_gather x5 -> x0, blocking collectives: 36.5 us -> none  [on_device(): slab_iter = lax.all_gather(current, 'grp', axis=0, tiled=True)]
    dot_general x8 -> x0, matrix products: 8.36 us -> none  [the longest x5 7.28 us: on_device(): product = jnp.dot(matrix, stacked, precision=lax.Precision.HIGHEST)]
    add x4 -> x0, other arithmetic: 6.32 us -> none  [the longest x1 4.99 us: smooth_last(): return values + 0.5 * (left_side + right_side)]
    slice x4 -> x0, local copies, waits for them, and re-layouts: 5.57 us -> none  [the longest x2 5.48 us: smooth_last(): jnp.roll(values, -1, axis=-1)]
  transfers between devices with their start and end apart: 15 -> 0, of which waited for: 15 -> 0; matrix products, arithmetic and copies ran while one was open for 0% -> 0% of each run, Pallas kernels for 0% -> 0%
where the time goes in v1:
time: 111 us
  Pallas kernels  84.2 us (76%)
  other arithmetic  24.3 us (22%)
  local copies, waits for them, and re-layouts  1.47 us (1%)
    pallas_call x1, Pallas kernels, on_device(): pl.pallas_call(functools.partial(sweep_kernel, subs), out_shape=jax.Shape...  60.6 us
    pallas_call x1, Pallas kernels, on_device(): pl.pallas_call(functools.partial(setup_kernel, subs, planes), out_shape=j...  23.6 us
    another operation x3, other arithmetic, on_device(): factor = jnp.linalg.cholesky(block)  12.4 us
    another operation x2, other arithmetic, on_device(): jax.scipy.linalg.cho_solve((factor, True), jnp.eye(rows, dtype=f32))  10.5 us

profile of v1, /device:TPU:17, one launch (start us, length us, event | category | flops | bytes accessed | tf_op | source)
XLA Modules:
  0.0 111.2 jit_solution(11801520851715480300)
XLA Ops:
  0.7 0.1 convert_select_fusion.pad_ref
  0.8 0.0 copy-start.2
  0.8 0.0 copy-start
  0.8 1.2 %bitcast_select_fusion.z_ref = bf16[512,512]{1,0:T(8,128)(2,1)S(1)} fusion(bf16[64,8,4,128]{3,2,1,0:T(4,128)(2,1)} %bitcast.21, pred[512]{0:T(512)(128)(4,1)S(1)} %iota_compare_fusion.3), kind=kLoop, calls=%fused_computation | loop fusion | flops 262144 | bytes 1049088 | tf_op jit(solution)/shard_map/jit(_where)/select_n | solution.py:315
  2.0 0.0 copy-done.2
  2.1 0.0 copy-done
  2.1 23.6 %coarse_rows.1.e_ref = f32[128,1536]{1,0:T(8,128)S(1)} custom-call(bf16[512,512]{1,0:T(8,128)(2,1)S(1)} %bitcast_select_fusion.z_ref, f32[8,512]{1,0:T(8,128)S(1)} %broadcast_in_dim.51.shift_ref, bf16[512,512]{1,0:T(8,128)(2,1)S(1)} %copy-done, f32[128,128]{1,0:T(8,128)S(1)} %convert_select_fusion.pad_ref), custom_call_target="tpu_custom_call" | custom-call | tf_op jit(solution)/shard_map/coarse_rows/pallas_call | solution.py:330
  25.7 0.1 copy.8
  25.8 11.7 %cholesky.13 = f32[128,128]{1,0:T(8,128)S(1)} custom-call(f32[128,128]{1,0:T(8,128)S(1)} %fusion.5), custom_call_target="Cholesky" | custom-call | tf_op jit(solution)/shard_map/jit(cholesky)/cholesky | solution.py:354
  37.6 0.6 compare_reduce_fusion
  38.2 0.7 fusion
  38.9 9.8 %custom-call.10 = f32[1,128,128]{1,2,0:T(8,128)S(1)} custom-call(f32[1,128,128]{2,1,0:T(8,128)S(1)} %fusion), custom_call_target="InvertDiagBlocksLowerTriangular" | custom-call | tf_op jit(solution)/shard_map/jit(_cho_solve)/triangular_solve | solution.py:355
  48.7 0.2 fusion.3
  49.0 0.0 copy-start.1
  49.0 0.2 fusion.1.inverse_ref
  49.2 0.7 copy-done.1
  49.9 0.1 broadcast_select_fusion.b_ref
  50.0 60.6 %sweeps.1 = f32[128,256]{1,0:T(8,128)S(1)} custom-call(f32[128,1536]{1,0:T(8,128)S(1)} %coarse_rows.1.e_ref, f32[128,128]{1,0:T(8,128)S(1)} %fusion.1.inverse_ref, f32[128,256]{1,0:T(8,128)S(1)} %broadcast_select_fusion.b_ref), custom_call_target="tpu_custom_call" | custom-call | tf_op jit(solution)/shard_map/sweeps/pallas_call | solution.py:358
  110.6 0.7 copy.13
  (6 shorter events, 0.1 us)
Async XLA Ops:
  0.8 1.3 %copy-start.2 = (f32[4,1,128]{2,1,0:T(1,128)S(1)}, f32[4,1,128]{2,1,0:T(1,128)}, u32[]{:S(2)}) copy-start(f32[4,1,128]{2,1,0:T(1,128)} %param.6) | copy-start | bytes 6148
  0.8 1.3 %copy-start = (bf16[512,512]{1,0:T(8,128)(2,1)S(1)}, bf16[512,512]{1,0:T(8,128)(2,1)}, u32[]{:S(2)}) copy-start(bf16[512,512]{1,0:T(8,128)(2,1)} %constant.67.clone.spread_ref) | copy-start | bytes 1572868
  49.0 0.9 copy-start.1

commit v2 on v1

--- a/solution.py
+++ b/solution.py
@@ -62,7 +62,7 @@
 
 
 def setup_kernel(
-    subs, planes, z_ref, shift_ref, spread_ref, pad_ref, e_ref,
+    subs, planes, z_ref, shift_ref, spread_ref, pad_ref, e_ref, inverse_ref,
     zall, rims, shifts, along, z_send, z_recv, rim_send, rim_recv, sh_send, sh_recv,
 ):
     s, g, far, near, corner, has_low, has_high = place(subs)
@@ -150,6 +150,7 @@
         def _(side=side):
             rim_copy(side, far, 3, near).wait_recv()
             rim_copy(side, far, 3, near).start()
+    inverse_of(e_ref[:, block], inverse_ref)
     for side in (0, 1):
         columns = pl.ds(2 * side * slots, slots)
 
@@ -193,114 +194,204 @@
                 rim_copy(side, g, kind, far).wait_send()
 
 
+def inverse_of(block, work):
+    n = block.shape[0]
+    size = 8
+    work[...] = block
+    lane = lax.broadcasted_iota(jnp.int32, (size, n), 1)
+    row = lax.broadcasted_iota(jnp.int32, (size, n), 0)
+    every_row = lax.broadcasted_iota(jnp.int32, (n, n), 0)
+    every_lane = lax.broadcasted_iota(jnp.int32, (n, n), 1)
+
+    def parts(values):
+        first = values.astype(jnp.bfloat16).astype(jnp.float32)
+        rest = values - first
+        second = rest.astype(jnp.bfloat16).astype(jnp.float32)
+        return first, second, rest - second
+
+    def panel(index, carry):
+        base = pl.multiple_of(index * size, size)
+        original = work[pl.ds(base, size), :]
+        columns = [
+            jnp.broadcast_to(
+                jnp.sum(jnp.where(lane == base + j, original, 0.0), axis=1, keepdims=True),
+                (size, n),
+            )
+            for j in range(size)
+        ]
+        values = original
+        for j in range(size):
+            factor = columns[j]
+            scale = 1.0 / factor[j : j + 1, :]
+            here = row == j
+
+            def eliminate(current):
+                pivot = current[j : j + 1, :] * scale
+                return jnp.where(here, pivot, current - factor * pivot)
+
+            unit = jnp.where(here, 1.0, 0.0)
+            values = eliminate(jnp.where(lane == base + j, unit, values))
+            for c in range(j + 1, size):
+                columns[c] = eliminate(columns[c])
+        inside = (lane >= base) & (lane < base + size)
+        left = jnp.where(inside, 0.0, jnp.where(lane < base, -original, original))
+        l1, l2, l3 = parts(left)
+        r1, r2, r3 = parts(values)
+        lefts = jnp.concatenate([l1, l1, l2, l2, l1, l3], axis=0).astype(jnp.bfloat16)
+        rights = jnp.concatenate([r1, r2, r1, r2, r3, r1], axis=0).astype(jnp.bfloat16)
+        product = lax.dot_general(
+            lefts, rights, (((0,), (0,)), ((), ())), preferred_element_type=jnp.float32
+        )
+        kept = jnp.where((every_lane >= base) & (every_lane < base + size), 0.0, work[...])
+        work[...] = kept - product
+        work[pl.ds(base, size), :] = values
+        return carry
+
+    lax.fori_loop(0, n // size, panel, 0)
+
+
 def sweep_kernel(
-    subs, e_ref, inverse_ref, b_ref, x_ref, matrix, held, change, sent, correction,
+    subs, e_ref, inverse_ref, b_ref, x_ref, matrix, held, sent, correction,
     send_sem, recv_sem,
 ):
     s, g, far, near, corner, has_low, has_high = place(subs)
     rows, width = b_ref.shape
-    groups = held.shape[1] // 3
+    groups = held.shape[2] // 3
+    halves = held.shape[1]
+    half = width // halves
     sends = {0: has_high, 1: has_low}
     holds = {0: has_low, 1: has_high}
     start = {0: 0, 1: 2 * groups}
     depth = groups * rows
 
-    def mix(at, kind, ref_slot, to):
-        ref = held.at[at, ref_slot]
-        return remote(ref, ref, send_sem.at[at, kind], recv_sem.at[at, ref_slot], to)
-
-    def first(at, side):
+    def mix(at, h, kind, slot, to):
+        ref = held.at[at, h, slot]
+        return remote(ref, ref, send_sem.at[at, h, kind], recv_sem.at[at, h, slot], to)
+
+    def first(at, h, side):
         to = s + 1 if side == 0 else s - 1
         slot = start[side] + g
         return remote(
-            held.at[at, groups + g], held.at[at, slot],
-            send_sem.at[at, side], recv_sem.at[at, slot], (to, g),
+            held.at[at, h, groups + g], held.at[at, h, slot],
+            send_sem.at[at, h, side], recv_sem.at[at, h, slot], (to, g),
         )
 
+    def cut(h):
+        return slice(h * half, (h + 1) * half)
+
+    def take(at, h, begin_slot):
+        values = held[at, h, pl.ds(begin_slot, groups)].reshape(depth, half)
+        columns = matrix[:, begin_slot * rows : (begin_slot + groups) * rows]
+        both = jnp.dot(columns, values, preferred_element_type=jnp.float32)
+        correction[:, cut(h)] = correction[:, cut(h)] - (both[0:rows] + both[rows:])
+
+    def send(at, h):
+        known = sent[:, cut(h)]
+        delta = (x_ref[:, cut(h)] - known).astype(jnp.bfloat16)
+        sent[:, cut(h)] = known + delta.astype(jnp.float32)
+        held[at, h, groups + g] = delta
+        for side in (0, 1):
+            @pl.when(sends[side])
+            def _(side=side):
+                first(at, h, side).start()
+        mix(at, h, 2, groups + g, (s, far)).start()
+        mix(at, h, 3, groups + g, (s, near)).start()
+
+    def pass_first(at, h):
+        mix(at, h, 4, groups + far, (s, near)).wait_recv()
+        mix(at, h, 4, groups + far, (s, near)).start()
+        for side in (0, 1):
+            @pl.when(holds[side])
+            def _(side=side):
+                slot = start[side] + g
+                mix(at, h, 5 + 3 * side, slot, (s, far)).wait_recv()
+                mix(at, h, 5 + 3 * side, slot, (s, far)).start()
+                mix(at, h, 6 + 3 * side, slot, (s, near)).start()
+
+    def pass_second(at, h):
+        for side in (0, 1):
+            @pl.when(holds[side])
+            def _(side=side):
+                slot = start[side] + far
+                mix(at, h, 7 + 3 * side, slot, (s, near)).wait_recv()
+                mix(at, h, 7 + 3 * side, slot, (s, near)).start()
+
+    def take_own(at, h):
+        for slot in (near, corner):
+            mix(at, h, 4, groups + slot, (s, near)).wait_recv()
+        take(at, h, groups)
+
+    def take_sides(at, h):
+        for side in (0, 1):
+            @pl.when(holds[side])
+            def _(side=side):
+                for other in (near, corner):
+                    mix(at, h, 7 + 3 * side, start[side] + other, (s, near)).wait_recv()
+                take(at, h, start[side])
+
+    def update(h):
+        x_ref[:, cut(h)] = x_ref[:, cut(h)] + damping * correction[:, cut(h)]
+
+    def sweep(at, last):
+        both = range(halves)
+        for h in both:
+            pass_first(at, h)
+        for h in both:
+            take_own(at, h)
+            pass_second(at, h)
+        for h in both:
+            take_sides(at, h)
+            update(h)
+            if not last:
+                send(at + 1, h)
+
     greet(s, g, far, near, has_low, has_high)
 
+    begin = jnp.dot(inverse_ref[...], b_ref[...], precision=HIGHEST,
+                    preferred_element_type=jnp.float32)
+    correction[...] = begin
+    x_ref[...] = damping * begin
+    sent[...] = jnp.zeros_like(sent)
+
+    starts = [(at, h) for at in (0, 1) for h in range(halves)]
+    for at, h in starts:
+        send(at, h)
     full = jnp.dot(inverse_ref[...], e_ref[...], precision=HIGHEST,
                    preferred_element_type=jnp.float32)
     high = full.astype(jnp.bfloat16)
     matrix[0:rows] = high
     matrix[rows : 2 * rows] = (full - high.astype(jnp.float32)).astype(jnp.bfloat16)
-    begin = jnp.dot(inverse_ref[...], b_ref[...], precision=HIGHEST,
-                    preferred_element_type=jnp.float32)
-    correction[...] = begin
-    x_ref[...] = damping * begin
-    sent[...] = jnp.zeros_like(sent)
-
-    def take(at, begin_slot):
-        values = held[at, pl.ds(begin_slot, groups)].reshape(depth, width)
-        columns = matrix[:, begin_slot * rows : (begin_slot + groups) * rows]
-        both = jnp.dot(columns, values, preferred_element_type=jnp.float32)
-        correction[...] = correction[...] - (both[0:rows] + both[rows:])
-
-    def send(at):
-        delta = (x_ref[...] - sent[...]).astype(jnp.bfloat16)
-        sent[...] = sent[...] + delta.astype(jnp.float32)
-        held[at, groups + g] = delta
-        for side in (0, 1):
-            @pl.when(sends[side])
-            def _(side=side):
-                first(at, side).start()
-        mix(at, 2, groups + g, (s, far)).start()
-        mix(at, 3, groups + g, (s, near)).start()
-
-    def collect(at):
-        mix(at, 4, groups + far, (s, near)).wait_recv()
-        mix(at, 4, groups + far, (s, near)).start()
-        for side in (0, 1):
-            @pl.when(holds[side])
-            def _(side=side):
-                slot = start[side] + g
-                mix(at, 5 + 3 * side, slot, (s, far)).wait_recv()
-                mix(at, 5 + 3 * side, slot, (s, far)).start()
-                mix(at, 6 + 3 * side, slot, (s, near)).start()
-        for slot in (near, corner):
-            mix(at, 4, groups + slot, (s, near)).wait_recv()
-        take(at, groups)
-        for side in (0, 1):
-            @pl.when(holds[side])
-            def _(side=side):
-                slot = start[side] + far
-                mix(at, 7 + 3 * side, slot, (s, near)).wait_recv()
-                mix(at, 7 + 3 * side, slot, (s, near)).start()
-        for side in (0, 1):
-            @pl.when(holds[side])
-            def _(side=side):
-                for other in (near, corner):
-                    mix(at, 7 + 3 * side, start[side] + other, (s, near)).wait_recv()
-                take(at, start[side])
-
-    def update():
-        x_ref[...] = x_ref[...] + damping * correction[...]
-
-    def sweep(at, carry):
-        send(at)
-        collect(at)
-        update()
+    for at, h in starts:
+        pass_first(at, h)
+    for at, h in starts:
+        take_own(at, h)
+        pass_second(at, h)
+    for h in range(halves):
+        take_sides(0, h)
+        take_sides(1, h)
+        update(h)
+        send(2, h)
+
+    def inner(at, carry):
+        sweep(at, False)
         return carry
 
-    send(0)
-    send(1)
-    collect(0)
-    collect(1)
-    update()
-    lax.fori_loop(2, SWEEPS, sweep, 0)
+    lax.fori_loop(2, SWEEPS - 1, inner, 0)
+    sweep(SWEEPS - 1, True)
 
     def drain(at, carry):
-        for kind in (2, 3, 4):
-            mix(at, kind, groups + g, (s, far)).wait_send()
-        for side in (0, 1):
-            @pl.when(sends[side])
-            def _(side=side):
-                first(at, side).wait_send()
-
-            @pl.when(holds[side])
-            def _(side=side):
-                for kind in (5, 6, 7):
-                    mix(at, kind + 3 * side, groups + g, (s, far)).wait_send()
+        for h in range(halves):
+            for kind in (2, 3, 4):
+                mix(at, h, kind, groups + g, (s, far)).wait_send()
+            for side in (0, 1):
+                @pl.when(sends[side])
+                def _(side=side):
+                    first(at, h, side).wait_send()
+
+                @pl.when(holds[side])
+                def _(side=side):
+                    for kind in (5, 6, 7):
+                        mix(at, h, kind + 3 * side, groups + g, (s, far)).wait_send()
         return carry
 
     lax.fori_loop(0, SWEEPS, drain, 0)
@@ -327,11 +418,14 @@
     vmem = pl.BlockSpec(memory_space=pltpu.VMEM)
     chunks = 4
     bf16, f32 = jnp.bfloat16, jnp.float32
-    matrix = pl.pallas_call(
+    matrix, inverse = pl.pallas_call(
         functools.partial(setup_kernel, subs, planes),
-        out_shape=jax.ShapeDtypeStruct((rows, 3 * slots), f32),
+        out_shape=(
+            jax.ShapeDtypeStruct((rows, 3 * slots), f32),
+            jax.ShapeDtypeStruct((rows, rows), f32),
+        ),
         in_specs=[vmem] * 4,
-        out_specs=vmem,
+        out_specs=(vmem, vmem),
         scratch_shapes=[
             pltpu.VMEM((groups, slots, cells), bf16),
             pltpu.VMEM((2, groups, slots, width), bf16),
@@ -350,11 +444,8 @@
         name="coarse_rows",
     )(masked, shift, spread, pad)
 
-    block = lax.dynamic_slice_in_dim(matrix, slots + lax.axis_index("grp") * rows, rows, 1)
-    factor = jnp.linalg.cholesky(block)
-    inverse = jax.scipy.linalg.cho_solve((factor, True), jnp.eye(rows, dtype=f32))
     rhs = jnp.where(dead[:, None], 0.0, right_sides)
-    count = SWEEPS
+    count, halves = SWEEPS, 2
     return pl.pallas_call(
         functools.partial(sweep_kernel, subs),
         out_shape=jax.ShapeDtypeStruct((rows, sides), f32),
@@ -362,12 +453,11 @@
         out_specs=vmem,
         scratch_shapes=[
             pltpu.VMEM((2 * rows, 3 * slots), bf16),
-            pltpu.VMEM((count, 3 * groups, rows, sides), bf16),
-            pltpu.VMEM((8, 128), f32),
+            pltpu.VMEM((count, halves, 3 * groups, rows, sides // halves), bf16),
             pltpu.VMEM((rows, sides), f32),
             pltpu.VMEM((rows, sides), f32),
-            pltpu.SemaphoreType.DMA((count, 11)),
-            pltpu.SemaphoreType.DMA((count, 3 * groups)),
+            pltpu.SemaphoreType.DMA((count, halves, 11)),
+            pltpu.SemaphoreType.DMA((count, halves, 3 * groups)),
         ],
         compiler_params=pltpu.CompilerParams(
             collective_id=1, has_side_effects=True, vmem_limit_bytes=40 * 2**20

time: 111 us -> 83.4 us (0.75)
  other arithmetic: 24.3 us -> 1.41 us
  Pallas kernels: 84.2 us -> 80.4 us
    another operation x5 -> x0, other arithmetic: 22.9 us -> none  [the longest x3 12.4 us: on_device(): factor = jnp.linalg.cholesky(block)]
    pallas_call x1, Pallas kernels: 60.6 us -> 54.5 us  [on_device(): pl.pallas_call(functools.partial(sweep_kernel, subs), out_shape=jax.Shape...]
    pallas_call x1, Pallas kernels: 23.6 us -> 25.9 us  [on_device(): pl.pallas_call(functools.partial(setup_kernel, subs, planes), out_shape=(...]
where the time goes in v2:
time: 83.4 us; the launch traced here: 83.3 us
  Pallas kernels  80.4 us (96%)
  other arithmetic  1.41 us (2%)
    pallas_call x1, Pallas kernels, on_device(): pl.pallas_call(functools.partial(sweep_kernel, subs), out_shape=jax.Shape...  54.5 us
    pallas_call x1, Pallas kernels, on_device(): pl.pallas_call(functools.partial(setup_kernel, subs, planes), out_shape=(...  25.9 us

profile of v2, /device:TPU:17, one launch (start us, length us, event | category | flops | bytes accessed | tf_op | source)
XLA Modules:
  0.0 83.3 jit_solution(13081241638608674989)
XLA Ops:
  0.7 0.1 convert_select_fusion.pad_ref
  0.8 0.0 copy-start.2
  0.8 0.0 copy-start
  0.8 1.2 %bitcast_select_fusion.z_ref = bf16[512,512]{1,0:T(8,128)(2,1)S(1)} fusion(bf16[64,8,4,128]{3,2,1,0:T(4,128)(2,1)} %bitcast.9, pred[512]{0:T(512)(128)(4,1)S(1)} %iota_compare_fusion.1), kind=kLoop, calls=%fused_computation | loop fusion | flops 262144 | bytes 1049088 | tf_op jit(solution)/shard_map/jit(_where)/select_n | solution.py:406
  2.0 0.0 copy-done.2
  2.1 0.0 copy-done
  2.1 0.0 copy-start.1
  2.1 25.9 %coarse_rows.1 = (f32[128,1536]{1,0:T(8,128)S(1)}, f32[128,128]{1,0:T(8,128)S(1)}) custom-call(bf16[512,512]{1,0:T(8,128)(2,1)S(1)} %bitcast_select_fusion.z_ref, f32[8,512]{1,0:T(8,128)S(1)} %broadcast_in_dim.49.shift_ref, bf16[512,512]{1,0:T(8,128)(2,1)S(1)} %copy-done, f32[128,128]{1,0:T(8,128)S(1)} %convert_select_fusion.pad_ref), custom_call_target="tpu_custom_call" | custom-call | tf_op jit(solution)/shard_map/coarse_rows/pallas_call | solution.py:421
  28.0 0.0 copy-done.1
  28.0 0.1 broadcast_select_fusion.b_ref
  28.1 54.5 %sweeps.1 = f32[128,256]{1,0:T(8,128)S(1)} custom-call(f32[128,1536]{1,0:T(8,128)S(1)} %get-tuple-element.7.e_ref, f32[128,128]{1,0:T(8,128)S(1)} %get-tuple-element.8.inverse_ref, f32[128,256]{1,0:T(8,128)S(1)} %broadcast_select_fusion.b_ref), custom_call_target="tpu_custom_call" | custom-call | tf_op jit(solution)/shard_map/sweeps/pallas_call | solution.py:449
  82.6 0.7 copy.10
  (3 shorter events, 0.0 us)
Async XLA Ops:
  0.8 1.3 %copy-start.2 = (f32[4,1,128]{2,1,0:T(1,128)S(1)}, f32[4,1,128]{2,1,0:T(1,128)}, u32[]{:S(2)}) copy-start(f32[4,1,128]{2,1,0:T(1,128)} %param.6) | copy-start | bytes 6148
  0.8 1.3 %copy-start = (bf16[512,512]{1,0:T(8,128)(2,1)S(1)}, bf16[512,512]{1,0:T(8,128)(2,1)}, u32[]{:S(2)}) copy-start(bf16[512,512]{1,0:T(8,128)(2,1)} %constant.12.clone.spread_ref) | copy-start | bytes 1572868
  2.1 25.9 %copy-start.1 = (f32[128,256]{1,0:T(8,128)S(1)}, f32[128,256]{1,0:T(8,128)}, u32[]{:S(2)}) copy-start(f32[128,256]{1,0:T(8,128)} %param.8) | copy-start | bytes 393220

commit v3 on v2

--- a/solution.py
+++ b/solution.py
@@ -61,11 +61,11 @@
     )
 
 
-def setup_kernel(
-    subs, planes, z_ref, shift_ref, spread_ref, pad_ref, e_ref, inverse_ref,
+def early_part(
+    planes, where, z_ref, shift_ref, spread_ref, pad_ref, e_ref, inverse_ref,
     zall, rims, shifts, along, z_send, z_recv, rim_send, rim_recv, sh_send, sh_recv,
 ):
-    s, g, far, near, corner, has_low, has_high = place(subs)
+    s, g, far, near, corner, has_low, has_high = where
     groups, slots, cells = zall.shape
     width = cells // planes
     own = slots // groups
@@ -77,7 +77,7 @@
     greet(s, g, far, near, has_low, has_high)
 
     def z_copy(slot, part, kind, to):
-        ref = zall.at[slot, pl.ds(part * step, step)]
+        ref = zall.at[slot, pl.ds(pl.multiple_of(part * step, step), step)]
         return remote(ref, ref, z_send.at[kind, part], z_recv.at[slot, part], (s, to))
 
     def sh_copy(slot, kind, to):
@@ -101,18 +101,44 @@
 
     sh_copy(g, 0, far).start()
     sh_copy(g, 1, near).start()
-    for part in range(chunks):
+    for part in (far, corner, g, near):
         z_copy(g, part, 0, far).start()
     for side in (0, 1):
         @pl.when(sends[side])
         def _(side=side):
             rim_first(side).start()
-    for part in range(chunks):
+    for part in (near, g, far, corner):
         z_copy(g, part, 1, near).start()
 
     sh_copy(far, 2, near).wait_recv()
     sh_copy(far, 2, near).start()
-    for part in range(chunks):
+    for part in (near, g):
+        z_copy(far, part, 2, near).wait_recv()
+        z_copy(far, part, 2, near).start()
+    sh_copy(near, 2, near).wait_recv()
+    sh_copy(corner, 2, near).wait_recv()
+    for slot in (near, corner):
+        z_copy(slot, g, 2, near).wait_recv()
+
+    def image_of(field, field_shift, lines, y):
+        beside = [lines[o] for o in (y - 1, y + 1) if 0 <= o < groups]
+        smooth = lines[y] + 0.5 * sum(beside[1:], beside[0]) if beside else lines[y]
+        centre = (16.0 + field_shift) * field.astype(jnp.float32)
+        return (centre - 2.0 * smooth).astype(jnp.bfloat16)
+
+    mine = pl.ds(pl.multiple_of(g * own, own), own)
+    lines = [
+        jnp.dot(zall[y, mine, :], spread_ref[...], preferred_element_type=jnp.float32)
+        for y in range(groups)
+    ]
+    diagonal = pad_ref[...]
+    for y in range(groups):
+        field = zall[y, mine, :]
+        diagonal = diagonal + against(field, image_of(field, shifts[y][0:1, :], lines, y))
+    inverse_ref[...] = diagonal
+    panels = own // 8
+    invert(inverse_ref, 0, panels // 3)
+    for part in (far, corner):
         z_copy(far, part, 2, near).wait_recv()
         z_copy(far, part, 2, near).start()
     for side in (0, 1):
@@ -121,36 +147,27 @@
             rim_copy(side, g, 1, far).wait_recv()
             rim_copy(side, g, 1, far).start()
             rim_copy(side, g, 2, near).start()
-
-    sh_copy(near, 2, near).wait_recv()
-    sh_copy(corner, 2, near).wait_recv()
-    for slot in (near, corner):
-        for part in range(chunks):
-            z_copy(slot, part, 2, near).wait_recv()
-
-    mine = pl.ds(pl.multiple_of(g * own, own), own)
-    for y in range(groups):
-        along[y] = jnp.dot(zall[y], spread_ref[...], preferred_element_type=jnp.float32)
-    total = jnp.zeros((own, slots), jnp.float32)
-    for y in range(groups):
-        beside = None
-        for other in (y - 1, y + 1):
-            if 0 <= other < groups:
-                beside = along[other] if beside is None else beside + along[other]
-        smooth = along[y] if beside is None else along[y] + 0.5 * beside
-        centre = (16.0 + shifts[y][0:1, :]) * zall[y].astype(jnp.float32)
-        image = (centre - 2.0 * smooth).astype(jnp.bfloat16)
-        total = total + against(zall[y, mine, :], image)
-    e_ref[:, pl.ds(slots, slots)] = total
-    block = pl.ds(pl.multiple_of(slots + g * own, own), own)
-    e_ref[:, block] = e_ref[:, block] + pad_ref[...]
+    invert(inverse_ref, panels // 3, panels)
+    yield
 
     for side in (0, 1):
         @pl.when(holds[side])
         def _(side=side):
             rim_copy(side, far, 3, near).wait_recv()
             rim_copy(side, far, 3, near).start()
-    inverse_of(e_ref[:, block], inverse_ref)
+    for slot in (near, corner):
+        for part in (near, far, corner):
+            z_copy(slot, part, 2, near).wait_recv()
+    for y in range(groups):
+        along[y] = jnp.dot(zall[y], spread_ref[...], preferred_element_type=jnp.float32)
+    total = jnp.zeros((own, slots), jnp.float32)
+    for y in range(groups):
+        image = image_of(zall[y], shifts[y][0:1, :], along, y)
+        total = total + against(zall[y, mine, :], image)
+    e_ref[:, pl.ds(slots, slots)] = total
+    block = pl.ds(pl.multiple_of(slots + g * own, own), own)
+    e_ref[:, block] = e_ref[:, block] + pad_ref[...]
+
     for side in (0, 1):
         columns = pl.ds(2 * side * slots, slots)
 
@@ -179,6 +196,8 @@
         def _(columns=columns):
             e_ref[:, columns] = jnp.zeros((own, slots), jnp.float32)
 
+    yield
+
     for kind in range(3):
         sh_copy(g, kind, far).wait_send()
         for part in range(chunks):
@@ -194,10 +213,9 @@
                 rim_copy(side, g, kind, far).wait_send()
 
 
-def inverse_of(block, work):
-    n = block.shape[0]
+def invert(work, begin, end):
+    n = work.shape[0]
     size = 8
-    work[...] = block
     lane = lax.broadcasted_iota(jnp.int32, (size, n), 1)
     row = lax.broadcasted_iota(jnp.int32, (size, n), 0)
     every_row = lax.broadcasted_iota(jnp.int32, (n, n), 0)
@@ -247,14 +265,15 @@
         work[pl.ds(base, size), :] = values
         return carry
 
-    lax.fori_loop(0, n // size, panel, 0)
-
-
-def sweep_kernel(
-    subs, e_ref, inverse_ref, b_ref, x_ref, matrix, held, sent, correction,
-    send_sem, recv_sem,
+    lax.fori_loop(begin, end, panel, 0)
+
+
+def kernel(
+    subs, planes, z_ref, shift_ref, spread_ref, pad_ref, b_ref, x_ref,
+    e_ref, inverse_ref, matrix, held, sent, correction, send_sem, recv_sem, *early_scratch,
 ):
-    s, g, far, near, corner, has_low, has_high = place(subs)
+    where = place(subs)
+    s, g, far, near, corner, has_low, has_high = where
     rows, width = b_ref.shape
     groups = held.shape[2] // 3
     halves = held.shape[1]
@@ -345,7 +364,10 @@
             if not last:
                 send(at + 1, h)
 
-    greet(s, g, far, near, has_low, has_high)
+    early = early_part(
+        planes, where, z_ref, shift_ref, spread_ref, pad_ref, e_ref, inverse_ref, *early_scratch
+    )
+    next(early)
 
     begin = jnp.dot(inverse_ref[...], b_ref[...], precision=HIGHEST,
                     preferred_element_type=jnp.float32)
@@ -356,6 +378,7 @@
     starts = [(at, h) for at in (0, 1) for h in range(halves)]
     for at, h in starts:
         send(at, h)
+    next(early)
     full = jnp.dot(inverse_ref[...], e_ref[...], precision=HIGHEST,
                    preferred_element_type=jnp.float32)
     high = full.astype(jnp.bfloat16)
@@ -395,6 +418,8 @@
         return carry
 
     lax.fori_loop(0, SWEEPS, drain, 0)
+    for _ in early:
+        pass
 
 
 def on_device(subs, groups, deflation, shift_field, counts, right_sides):
@@ -416,23 +441,29 @@
     dead = row_slot >= live_count
     pad = jnp.where(dead[:, None], jnp.eye(rows, dtype=jnp.float32), 0.0)
     vmem = pl.BlockSpec(memory_space=pltpu.VMEM)
-    chunks = 4
     bf16, f32 = jnp.bfloat16, jnp.float32
-    matrix, inverse = pl.pallas_call(
-        functools.partial(setup_kernel, subs, planes),
-        out_shape=(
-            jax.ShapeDtypeStruct((rows, 3 * slots), f32),
-            jax.ShapeDtypeStruct((rows, rows), f32),
-        ),
-        in_specs=[vmem] * 4,
-        out_specs=(vmem, vmem),
+    rhs = jnp.where(dead[:, None], 0.0, right_sides)
+    count, halves = SWEEPS, 2
+    return pl.pallas_call(
+        functools.partial(kernel, subs, planes),
+        out_shape=jax.ShapeDtypeStruct((rows, sides), f32),
+        in_specs=[vmem] * 5,
+        out_specs=vmem,
         scratch_shapes=[
+            pltpu.VMEM((rows, 3 * slots), f32),
+            pltpu.VMEM((rows, rows), f32),
+            pltpu.VMEM((2 * rows, 3 * slots), bf16),
+            pltpu.VMEM((count, halves, 3 * groups, rows, sides // halves), bf16),
+            pltpu.VMEM((rows, sides), f32),
+            pltpu.VMEM((rows, sides), f32),
+            pltpu.SemaphoreType.DMA((count, halves, 11)),
+            pltpu.SemaphoreType.DMA((count, halves, 3 * groups)),
             pltpu.VMEM((groups, slots, cells), bf16),
             pltpu.VMEM((2, groups, slots, width), bf16),
             pltpu.VMEM((groups, 8, cells), f32),
             pltpu.VMEM((groups, slots, cells), f32),
-            pltpu.SemaphoreType.DMA((3, chunks)),
-            pltpu.SemaphoreType.DMA((groups, chunks)),
+            pltpu.SemaphoreType.DMA((3, groups)),
+            pltpu.SemaphoreType.DMA((groups, groups)),
             pltpu.SemaphoreType.DMA((2, 4)),
             pltpu.SemaphoreType.DMA((2, groups)),
             pltpu.SemaphoreType.DMA((3,)),
@@ -441,29 +472,8 @@
         compiler_params=pltpu.CompilerParams(
             collective_id=0, has_side_effects=True, vmem_limit_bytes=40 * 2**20
         ),
-        name="coarse_rows",
-    )(masked, shift, spread, pad)
-
-    rhs = jnp.where(dead[:, None], 0.0, right_sides)
-    count, halves = SWEEPS, 2
-    return pl.pallas_call(
-        functools.partial(sweep_kernel, subs),
-        out_shape=jax.ShapeDtypeStruct((rows, sides), f32),
-        in_specs=[vmem] * 3,
-        out_specs=vmem,
-        scratch_shapes=[
-            pltpu.VMEM((2 * rows, 3 * slots), bf16),
-            pltpu.VMEM((count, halves, 3 * groups, rows, sides // halves), bf16),
-            pltpu.VMEM((rows, sides), f32),
-            pltpu.VMEM((rows, sides), f32),
-            pltpu.SemaphoreType.DMA((count, halves, 11)),
-            pltpu.SemaphoreType.DMA((count, halves, 3 * groups)),
-        ],
-        compiler_params=pltpu.CompilerParams(
-            collective_id=1, has_side_effects=True, vmem_limit_bytes=40 * 2**20
-        ),
-        name="sweeps",
-    )(matrix, inverse, rhs)
+        name="schwarz",
+    )(masked, shift, spread, pad, rhs)
 
 
 def solution(mesh):

time: 83.4 us -> 78.3 us (0.939)
  Pallas kernels: 80.4 us -> 73.1 us
  other arithmetic: 1.41 us -> 2.32 us
    pallas_call x2 -> x1, Pallas kernels: 80.4 us -> 73.1 us  [on_device(): pl.pallas_call(functools.partial(kernel, subs, planes), out_shape=jax.Sha...]
    select_n x1, other arithmetic: 0.08 us -> 0.99 us  [on_device(): rhs = jnp.where(dead[:, None], 0.0, right_sides)]
where the time goes in v3:
time: 78.3 us; the launch traced here: 77.4 us
  Pallas kernels  73.1 us (93%)
  other arithmetic  2.32 us (3%)
  local copies, waits for them, and re-layouts  1.33 us (2%)
    pallas_call x1, Pallas kernels, on_device(): pl.pallas_call(functools.partial(kernel, subs, planes), out_shape=jax.Sha...  73.1 us

profile of v3, /device:TPU:17, one launch (start us, length us, event | category | flops | bytes accessed | tf_op | source)
XLA Modules:
  0.0 77.4 jit_solution(2468577407948355485)
XLA Ops:
  0.7 0.0 copy-start.1
  0.7 0.7 copy-done.1
  1.4 0.1 convert_select_fusion.pad_ref
  1.4 1.0 %broadcast_select_fusion.b_ref = f32[128,256]{1,0:T(8,128)S(1)} fusion(f32[128,256]{1,0:T(8,128)} %param.8, pred[128]{0:T(512)(128)(4,1)S(1)} %add_compare_fusion), kind=kLoop, calls=%fused_computation.1 | loop fusion | flops 32768 | bytes 262272 | tf_op jit(solution)/shard_map/jit(_where)/select_n | solution.py:445
  2.4 0.0 copy-start
  2.5 1.2 %bitcast_select_fusion.z_ref = bf16[512,512]{1,0:T(8,128)(2,1)S(1)} fusion(bf16[64,8,4,128]{3,2,1,0:T(4,128)(2,1)} %bitcast.9, pred[512]{0:T(512)(128)(4,1)S(1)} %iota_compare_fusion.1), kind=kLoop, calls=%fused_computation | loop fusion | flops 262144 | bytes 1049088 | tf_op jit(solution)/shard_map/jit(_where)/select_n | solution.py:431
  3.7 0.0 copy-done
  3.7 73.1 %schwarz.1 = f32[128,256]{1,0:T(8,128)S(1)} custom-call(bf16[512,512]{1,0:T(8,128)(2,1)S(1)} %bitcast_select_fusion.z_ref, f32[8,512]{1,0:T(8,128)S(1)} %broadcast_in_dim.49.shift_ref, bf16[512,512]{1,0:T(8,128)(2,1)S(1)} %copy-done, f32[128,128]{1,0:T(8,128)S(1)} %convert_select_fusion.pad_ref, f32[128,256]{1,0:T(8,128)S(1)} %broadcast_select_fusion.b_ref), custom_call_target="tpu_custom_call" | custom-call | tf_op jit(solution)/shard_map/schwarz/pallas_call | solution.py:447
  76.8 0.7 copy.10
  (3 shorter events, 0.0 us)
Async XLA Ops:
  0.7 0.7 copy-start.1
  2.4 1.3 %copy-start = (bf16[512,512]{1,0:T(8,128)(2,1)S(1)}, bf16[512,512]{1,0:T(8,128)(2,1)}, u32[]{:S(2)}) copy-start(bf16[512,512]{1,0:T(8,128)(2,1)} %constant.12.clone.spread_ref) | copy-start | bytes 1572868

commit v4 on v3

--- a/solution.py
+++ b/solution.py
@@ -302,24 +302,27 @@
         values = held[at, h, pl.ds(begin_slot, groups)].reshape(depth, half)
         columns = matrix[:, begin_slot * rows : (begin_slot + groups) * rows]
         both = jnp.dot(columns, values, preferred_element_type=jnp.float32)
-        correction[:, cut(h)] = correction[:, cut(h)] - (both[0:rows] + both[rows:])
-
-    def send(at, h):
+        product = both[0:rows] + both[rows:]
+        correction[:, cut(h)] = correction[:, cut(h)] - product
+        return product
+
+    def send(at, h, wide=True):
         known = sent[:, cut(h)]
         delta = (x_ref[:, cut(h)] - known).astype(jnp.bfloat16)
-        sent[:, cut(h)] = known + delta.astype(jnp.float32)
+        if wide:
+            sent[:, cut(h)] = known + delta.astype(jnp.float32)
         held[at, h, groups + g] = delta
-        for side in (0, 1):
+        for side in (0, 1) if wide else ():
             @pl.when(sends[side])
             def _(side=side):
                 first(at, h, side).start()
         mix(at, h, 2, groups + g, (s, far)).start()
         mix(at, h, 3, groups + g, (s, near)).start()
 
-    def pass_first(at, h):
+    def pass_first(at, h, wide=True):
         mix(at, h, 4, groups + far, (s, near)).wait_recv()
         mix(at, h, 4, groups + far, (s, near)).start()
-        for side in (0, 1):
+        for side in (0, 1) if wide else ():
             @pl.when(holds[side])
             def _(side=side):
                 slot = start[side] + g
@@ -338,7 +341,7 @@
     def take_own(at, h):
         for slot in (near, corner):
             mix(at, h, 4, groups + slot, (s, near)).wait_recv()
-        take(at, h, groups)
+        return take(at, h, groups)
 
     def take_sides(at, h):
         for side in (0, 1):
@@ -369,7 +372,8 @@
     )
     next(early)
 
-    begin = jnp.dot(inverse_ref[...], b_ref[...], precision=HIGHEST,
+    live = 1.0 - jnp.sum(pad_ref[...], axis=0, keepdims=True)
+    begin = jnp.dot(inverse_ref[...] * live, b_ref[...], precision=HIGHEST,
                     preferred_element_type=jnp.float32)
     correction[...] = begin
     x_ref[...] = damping * begin
@@ -377,7 +381,7 @@
 
     starts = [(at, h) for at in (0, 1) for h in range(halves)]
     for at, h in starts:
-        send(at, h)
+        send(at, h, at == 0)
     next(early)
     full = jnp.dot(inverse_ref[...], e_ref[...], precision=HIGHEST,
                    preferred_element_type=jnp.float32)
@@ -385,14 +389,17 @@
     matrix[0:rows] = high
     matrix[rows : 2 * rows] = (full - high.astype(jnp.float32)).astype(jnp.bfloat16)
     for at, h in starts:
-        pass_first(at, h)
-    for at, h in starts:
-        take_own(at, h)
-        pass_second(at, h)
+        pass_first(at, h, at == 0)
+    rest = []
+    for h in range(halves):
+        take_own(0, h)
+        pass_second(0, h)
+    for h in range(halves):
+        rest.append(take_own(1, h))
     for h in range(halves):
         take_sides(0, h)
-        take_sides(1, h)
         update(h)
+        correction[:, cut(h)] = correction[:, cut(h)] + rest[h]
         send(2, h)
 
     def inner(at, carry):
@@ -402,11 +409,11 @@
     lax.fori_loop(2, SWEEPS - 1, inner, 0)
     sweep(SWEEPS - 1, True)
 
-    def drain(at, carry):
+    def drain(at, wide=True):
         for h in range(halves):
             for kind in (2, 3, 4):
                 mix(at, h, kind, groups + g, (s, far)).wait_send()
-            for side in (0, 1):
+            for side in (0, 1) if wide else ():
                 @pl.when(sends[side])
                 def _(side=side):
                     first(at, h, side).wait_send()
@@ -415,9 +422,14 @@
                 def _(side=side):
                     for kind in (5, 6, 7):
                         mix(at, h, kind + 3 * side, groups + g, (s, far)).wait_send()
+
+    def drained(at, carry):
+        drain(at)
         return carry
 
-    lax.fori_loop(0, SWEEPS, drain, 0)
+    drain(0)
+    drain(1, False)
+    lax.fori_loop(2, SWEEPS, drained, 0)
     for _ in early:
         pass
 
@@ -442,7 +454,6 @@
     pad = jnp.where(dead[:, None], jnp.eye(rows, dtype=jnp.float32), 0.0)
     vmem = pl.BlockSpec(memory_space=pltpu.VMEM)
     bf16, f32 = jnp.bfloat16, jnp.float32
-    rhs = jnp.where(dead[:, None], 0.0, right_sides)
     count, halves = SWEEPS, 2
     return pl.pallas_call(
         functools.partial(kernel, subs, planes),
@@ -473,7 +484,7 @@
             collective_id=0, has_side_effects=True, vmem_limit_bytes=40 * 2**20
         ),
         name="schwarz",
-    )(masked, shift, spread, pad, rhs)
+    )(masked, shift, spread, pad, right_sides)
 
 
 def solution(mesh):

time: 78.3 us -> 75.4 us (0.963)
  Pallas kernels: 73.1 us -> 70.5 us
  other arithmetic: 2.32 us -> 1.33 us
    pallas_call x1, Pallas kernels: 73.1 us -> 70.5 us  [on_device(): pl.pallas_call(functools.partial(kernel, subs, planes), out_shape=jax.Sha...]
    select_n x1 -> x0, other arithmetic: 0.99 us -> none  [on_device(): rhs = jnp.where(dead[:, None], 0.0, right_sides)]
where the time goes in v4:
time: 75.4 us; the launch traced here: 73.9 us
  Pallas kernels  70.5 us (94%)
  local copies, waits for them, and re-layouts  1.34 us (2%)
  other arithmetic  1.33 us (2%)
    pallas_call x1, Pallas kernels, on_device(): pl.pallas_call(functools.partial(kernel, subs, planes), out_shape=jax.Sha...  70.5 us

profile of v4, /device:TPU:17, one launch (start us, length us, event | category | flops | bytes accessed | tf_op | source)
XLA Modules:
  0.0 73.9 jit_solution(4963995634319498362)
XLA Ops:
  0.7 0.0 copy-start.2
  0.7 0.7 copy-done.2
  1.4 0.1 convert_select_fusion.pad_ref
  1.4 0.0 copy-start
  1.5 0.0 copy-start.1
  1.5 1.2 %bitcast_select_fusion.z_ref = bf16[512,512]{1,0:T(8,128)(2,1)S(1)} fusion(bf16[64,8,4,128]{3,2,1,0:T(4,128)(2,1)} %bitcast.9, pred[512]{0:T(512)(128)(4,1)S(1)} %iota_compare_fusion.1), kind=kLoop, calls=%fused_computation | loop fusion | flops 262144 | bytes 1049088 | tf_op jit(solution)/shard_map/jit(_where)/select_n | solution.py:443
  2.7 0.0 copy-done
  2.7 0.0 copy-done.1
  2.7 70.5 %schwarz.1 = f32[128,256]{1,0:T(8,128)S(1)} custom-call(bf16[512,512]{1,0:T(8,128)(2,1)S(1)} %bitcast_select_fusion.z_ref, f32[8,512]{1,0:T(8,128)S(1)} %broadcast_in_dim.36.shift_ref, bf16[512,512]{1,0:T(8,128)(2,1)S(1)} %copy-done, f32[128,128]{1,0:T(8,128)S(1)} %convert_select_fusion.pad_ref, f32[128,256]{1,0:T(8,128)S(1)} %copy-done.1), custom_call_target="tpu_custom_call" | custom-call | tf_op jit(solution)/shard_map/schwarz/pallas_call | solution.py:458
  73.3 0.7 copy.10
  (3 shorter events, 0.0 us)
Async XLA Ops:
  0.7 0.7 copy-start.2
  1.4 1.3 %copy-start = (bf16[512,512]{1,0:T(8,128)(2,1)S(1)}, bf16[512,512]{1,0:T(8,128)(2,1)}, u32[]{:S(2)}) copy-start(bf16[512,512]{1,0:T(8,128)(2,1)} %constant.12.clone.spread_ref) | copy-start | bytes 1572868
  1.5 1.3 %copy-start.1 = (f32[128,256]{1,0:T(8,128)S(1)}, f32[128,256]{1,0:T(8,128)}, u32[]{:S(2)}) copy-start(f32[128,256]{1,0:T(8,128)} %b_ref.1) | copy-start | bytes 393220

commit v5 on v4

--- a/solution.py
+++ b/solution.py
@@ -359,8 +359,8 @@
         for h in both:
             pass_first(at, h)
         for h in both:
+            pass_second(at, h)
             take_own(at, h)
-            pass_second(at, h)
         for h in both:
             take_sides(at, h)
             update(h)

time: 75.4 us -> 75.3 us (level); the launches traced: 73.9 us -> 74.8 us
  Pallas kernels: 70.5 us -> 71.4 us
    pallas_call x1, Pallas kernels: 70.5 us -> 71.4 us  [on_device(): pl.pallas_call(functools.partial(kernel, subs, planes), out_shape=jax.Sha...]
where the time goes in v5:
time: 75.3 us; the launch traced here: 74.8 us
  Pallas kernels  71.4 us (95%)
  local copies, waits for them, and re-layouts  1.34 us (2%)
  other arithmetic  1.33 us (2%)
    pallas_call x1, Pallas kernels, on_device(): pl.pallas_call(functools.partial(kernel, subs, planes), out_shape=jax.Sha...  71.4 us

profile of v5, /device:TPU:17, one launch (start us, length us, event | category | flops | bytes accessed | tf_op | source)
XLA Modules:
  0.0 74.8 jit_solution(2746673489487865916)
XLA Ops:
  0.7 0.0 copy-start.2
  0.7 0.7 copy-done.2
  1.4 0.1 convert_select_fusion.pad_ref
  1.4 0.0 copy-start
  1.5 0.0 copy-start.1
  1.5 1.2 %bitcast_select_fusion.z_ref = bf16[512,512]{1,0:T(8,128)(2,1)S(1)} fusion(bf16[64,8,4,128]{3,2,1,0:T(4,128)(2,1)} %bitcast.9, pred[512]{0:T(512)(128)(4,1)S(1)} %iota_compare_fusion.1), kind=kLoop, calls=%fused_computation | loop fusion | flops 262144 | bytes 1049088 | tf_op jit(solution)/shard_map/jit(_where)/select_n | solution.py:443
  2.7 0.0 copy-done
  2.7 0.0 copy-done.1
  2.7 71.4 %schwarz.1 = f32[128,256]{1,0:T(8,128)S(1)} custom-call(bf16[512,512]{1,0:T(8,128)(2,1)S(1)} %bitcast_select_fusion.z_ref, f32[8,512]{1,0:T(8,128)S(1)} %broadcast_in_dim.36.shift_ref, bf16[512,512]{1,0:T(8,128)(2,1)S(1)} %copy-done, f32[128,128]{1,0:T(8,128)S(1)} %convert_select_fusion.pad_ref, f32[128,256]{1,0:T(8,128)S(1)} %copy-done.1), custom_call_target="tpu_custom_call" | custom-call | tf_op jit(solution)/shard_map/schwarz/pallas_call | solution.py:458
  74.2 0.7 copy.10
  (3 shorter events, 0.0 us)
Async XLA Ops:
  0.7 0.7 copy-start.2
  1.4 1.3 %copy-start = (bf16[512,512]{1,0:T(8,128)(2,1)S(1)}, bf16[512,512]{1,0:T(8,128)(2,1)}, u32[]{:S(2)}) copy-start(bf16[512,512]{1,0:T(8,128)(2,1)} %constant.12.clone.spread_ref) | copy-start | bytes 1572868
  1.5 1.3 %copy-start.1 = (f32[128,256]{1,0:T(8,128)S(1)}, f32[128,256]{1,0:T(8,128)}, u32[]{:S(2)}) copy-start(f32[128,256]{1,0:T(8,128)} %b_ref.1) | copy-start | bytes 393220

commit v6 on v5

--- a/solution.py
+++ b/solution.py
@@ -46,12 +46,14 @@
     @pl.when(has_low)
     def _():
         signal((s - 1, g))
+        signal((s - 1, far))
 
     @pl.when(has_high)
     def _():
         signal((s + 1, g))
-
-    peers = 2 + has_low.astype(jnp.int32) + has_high.astype(jnp.int32)
+        signal((s + 1, far))
+
+    peers = 2 + 2 * has_low.astype(jnp.int32) + 2 * has_high.astype(jnp.int32)
     pl.semaphore_wait(barrier, peers)
 
 
@@ -287,12 +289,12 @@
         ref = held.at[at, h, slot]
         return remote(ref, ref, send_sem.at[at, h, kind], recv_sem.at[at, h, slot], to)
 
-    def first(at, h, side):
+    def first(at, h, side, kind, to_grp):
         to = s + 1 if side == 0 else s - 1
         slot = start[side] + g
         return remote(
             held.at[at, h, groups + g], held.at[at, h, slot],
-            send_sem.at[at, h, side], recv_sem.at[at, h, slot], (to, g),
+            send_sem.at[at, h, kind], recv_sem.at[at, h, slot], (to, to_grp),
         )
 
     def cut(h):
@@ -315,7 +317,8 @@
         for side in (0, 1) if wide else ():
             @pl.when(sends[side])
             def _(side=side):
-                first(at, h, side).start()
+                first(at, h, side, side, g).start()
+                first(at, h, side, 5 + 3 * side, far).start()
         mix(at, h, 2, groups + g, (s, far)).start()
         mix(at, h, 3, groups + g, (s, near)).start()
 
@@ -326,8 +329,7 @@
             @pl.when(holds[side])
             def _(side=side):
                 slot = start[side] + g
-                mix(at, h, 5 + 3 * side, slot, (s, far)).wait_recv()
-                mix(at, h, 5 + 3 * side, slot, (s, far)).start()
+                mix(at, h, 6 + 3 * side, slot, (s, near)).wait_recv()
                 mix(at, h, 6 + 3 * side, slot, (s, near)).start()
 
     def pass_second(at, h):
@@ -416,11 +418,12 @@
             for side in (0, 1) if wide else ():
                 @pl.when(sends[side])
                 def _(side=side):
-                    first(at, h, side).wait_send()
+                    first(at, h, side, side, g).wait_send()
+                    first(at, h, side, 5 + 3 * side, far).wait_send()
 
                 @pl.when(holds[side])
                 def _(side=side):
-                    for kind in (5, 6, 7):
+                    for kind in (6, 7):
                         mix(at, h, kind + 3 * side, groups + g, (s, far)).wait_send()
 
     def drained(at, carry):

time: 75.3 us -> 73.6 us (0.977)
  Pallas kernels: 71.4 us -> 70 us
    pallas_call x1, Pallas kernels: 71.4 us -> 70 us  [on_device(): pl.pallas_call(functools.partial(kernel, subs, planes), out_shape=jax.Sha...]
where the time goes in v6:
time: 73.6 us; the launch traced here: 73.4 us
  Pallas kernels  70 us (95%)
  local copies, waits for them, and re-layouts  1.34 us (2%)
  other arithmetic  1.33 us (2%)
    pallas_call x1, Pallas kernels, on_device(): pl.pallas_call(functools.partial(kernel, subs, planes), out_shape=jax.Sha...  70 us

profile of v6, /device:TPU:17, one launch (start us, length us, event | category | flops | bytes accessed | tf_op | source)
XLA Modules:
  0.0 73.4 jit_solution(12215791865167852898)
XLA Ops:
  0.7 0.0 copy-start.2
  0.7 0.7 copy-done.2
  1.4 0.1 convert_select_fusion.pad_ref
  1.4 0.0 copy-start
  1.5 0.0 copy-start.1
  1.5 1.2 %bitcast_select_fusion.z_ref = bf16[512,512]{1,0:T(8,128)(2,1)S(1)} fusion(bf16[64,8,4,128]{3,2,1,0:T(4,128)(2,1)} %bitcast.9, pred[512]{0:T(512)(128)(4,1)S(1)} %iota_compare_fusion.1), kind=kLoop, calls=%fused_computation | loop fusion | flops 262144 | bytes 1049088 | tf_op jit(solution)/shard_map/jit(_where)/select_n | solution.py:446
  2.7 0.0 copy-done
  2.7 0.0 copy-done.1
  2.7 70.0 %schwarz.1 = f32[128,256]{1,0:T(8,128)S(1)} custom-call(bf16[512,512]{1,0:T(8,128)(2,1)S(1)} %bitcast_select_fusion.z_ref, f32[8,512]{1,0:T(8,128)S(1)} %broadcast_in_dim.36.shift_ref, bf16[512,512]{1,0:T(8,128)(2,1)S(1)} %copy-done, f32[128,128]{1,0:T(8,128)S(1)} %convert_select_fusion.pad_ref, f32[128,256]{1,0:T(8,128)S(1)} %copy-done.1), custom_call_target="tpu_custom_call" | custom-call | tf_op jit(solution)/shard_map/schwarz/pallas_call | solution.py:461
  72.8 0.7 copy.10
  (3 shorter events, 0.0 us)
Async XLA Ops:
  0.7 0.7 copy-start.2
  1.4 1.3 %copy-start = (bf16[512,512]{1,0:T(8,128)(2,1)S(1)}, bf16[512,512]{1,0:T(8,128)(2,1)}, u32[]{:S(2)}) copy-start(bf16[512,512]{1,0:T(8,128)(2,1)} %constant.12.clone.spread_ref) | copy-start | bytes 1572868
  1.5 1.3 %copy-start.1 = (f32[128,256]{1,0:T(8,128)S(1)}, f32[128,256]{1,0:T(8,128)}, u32[]{:S(2)}) copy-start(f32[128,256]{1,0:T(8,128)} %b_ref.1) | copy-start | bytes 393220
